TPU v7x, 128 devices: a whole 4x4x4 slice. The times are simulated.
128 devices in a mesh: dp: 16 (over y_lo, x, core), space: 8 (over z, y_hi).
Axes of the slice: x: 4, y: 4 (y_hi: 2, y_lo: 2; y = y_hi * 2 + y_lo), z: 4, core: 2. Of those that a mesh axis runs over, the one named last changes fastest.
Arguments:
- inputs: bfloat16 [16, 1, 64, 240, 320], P('dp', None, 'space'), may hold values from -6 to 6
- preacts: bfloat16 [1, 16, 1, 64, 240, 320], P(None, 'dp', None, 'space'), may hold values from -6 to 6
- cotangent: bfloat16 [16, 1, 64, 240, 320], P('dp', None, 'space'), may hold values from -0.01171875 to 0.01171875
- weights: bfloat16 [1, 2880, 320], replicated, may hold values from -0.109375 to 0.109375
- left_stats: float32 [2, 2880, 2880], P(None, 'space', 'dp'), as said below
- left_basis: float32 [2, 2880, 320], P(None, 'dp'), may hold values from -6 to 6
- right_stats: float32 [2, 320, 320], replicated, as said below
- right_basis: float32 [2, 320, 320], replicated, as said below
Outputs:
- left_out: float32 [2, 2880, 2880], P(None, 'space', 'dp')
- basis_out: float32 [2, 2880, 320], replicated
- right_out: float32 [2, 320, 320], replicated
- right_basis_out: float32 [2, 320, 320], replicated
Inputs may be any that keep to these rules, and one draw needn't show every extreme that they name: `left_stats`: each matrix is symmetric positive definite. `right_stats`: each matrix is symmetric positive definite. `right_basis`: each matrix is invertible.
All inputs are finite; a program needn't handle non-finite values.
Results may differ from a plain program's by a relative error of at most 0.0014.
Values may be sent and summed in bfloat16 or wider, within the bound.
A program may use at most 128 MiB of HBM per device.

v0:
```python
import math

import jax
import jax.numpy as jnp
from jax import lax
from jax.sharding import PartitionSpec as P

BETA = 0.95
HIGHEST = lax.Precision.HIGHEST
OFFSETS = (-1, 0, 1)
CONTRACT_ROWS = (((0,), (0,)), ((), ()))
CONTRACT_COLS = (((1,), (1,)), ((), ()))


def padded_2(array, sides, width):
    for axis, dim in sides:
        size, length = (lax.axis_size(axis), array.shape[dim])
        up = [(i, (i + 1) % size) for i in range(size - 1)]
        down = [(j, i) for i, j in up]
        last = lax.slice_in_dim(array, length - width, length, axis=dim)
        first = lax.slice_in_dim(array, 0, width, axis=dim)
        before = lax.ppermute(last, axis, up)
        after = lax.ppermute(first, axis, down)
        array = jnp.concatenate([before, array, after], axis=dim)
    return array


def silu_slope(preact):
    argument = preact.astype(jnp.float32)
    logistic = jax.nn.sigmoid(argument)
    return logistic * (1.0 + argument * (1.0 - logistic))


def widen(with_rows):
    return jnp.pad(with_rows, ((0, 0), (0, 0), (0, 0), (1, 1), (0, 0)))


def weight_grad(input_rims, layer_grad):
    row_count, col_count, channels = (layer_grad.shape[2], layer_grad.shape[3], layer_grad.shape[4])
    padded = widen(input_rims)
    flat_grad = layer_grad.reshape(-1, channels)
    blocks = []
    for row_step in OFFSETS:
        for col_step in OFFSETS:
            shifted = padded[
                :,
                :,
                1 + row_step : 1 + row_step + row_count,
                1 + col_step : 1 + col_step + col_count,
                :,
            ]
            blocks.append(
                lax.dot_general(
                    shifted.reshape(-1, channels),
                    flat_grad,
                    CONTRACT_ROWS,
                    preferred_element_type=jnp.float32,
                )
            )
    return jnp.concatenate(blocks, axis=0)


def input_grad(grad_rims, weight):
    row_count = grad_rims.shape[2] - 2
    col_count, channels = (grad_rims.shape[3], grad_rims.shape[4])
    padded = widen(grad_rims)
    summed = jnp.zeros(
        (grad_rims.shape[0] * grad_rims.shape[1] * row_count * col_count, channels), jnp.float32
    )
    tap_number = 0
    for row_step in OFFSETS:
        for col_step in OFFSETS:
            shifted = padded[
                :,
                :,
                1 - row_step : 1 - row_step + row_count,
                1 - col_step : 1 - col_step + col_count,
                :,
            ]
            weight_tap = weight[tap_number * channels : (tap_number + 1) * channels]
            summed = summed + lax.dot_general(
                shifted.reshape(-1, channels),
                weight_tap,
                CONTRACT_COLS,
                preferred_element_type=jnp.float32,
            )
            tap_number += 1
    return summed.reshape(grad_rims.shape[0], grad_rims.shape[1], row_count, col_count, channels)


def orthonormal(product_rows, gram_matrix, factor):
    lower_factor = jnp.linalg.cholesky(gram_matrix)
    solved = jax.scipy.linalg.solve_triangular(lower_factor, product_rows.T, lower=True)
    return solved.T * factor


def with_rims(stacked):
    return padded_2(stacked, (("space", 3),), 1)


def local(inputs, preacts, cotangent, weights, left_stats, left_basis, right_stats, right_basis):
    layer_total = left_stats.shape[0]
    row_share = left_stats.shape[1]
    col_share = left_stats.shape[2]
    channels = inputs.shape[-1]
    full_rows = weights.shape[1]
    dp_index = lax.axis_index("dp")
    space_index = lax.axis_index("space")
    layer_inputs = [inputs] + [jax.nn.silu(preacts[0].astype(jnp.float32)).astype(jnp.bfloat16)]
    left_outs = [None] * layer_total
    basis_outs = [None] * layer_total
    right_outs = [None] * layer_total
    turned_outs = [None] * layer_total

    def finish(layer_num, product_rows, gram_left, gram_right):
        basis_rows = orthonormal(product_rows, gram_left, math.sqrt(full_rows))
        basis_outs[layer_num] = lax.all_gather(basis_rows, "space", axis=0, tiled=True)
        right_new = BETA * right_stats[layer_num] + (1.0 - BETA) * gram_right
        right_rows = jnp.dot(right_new, right_basis[layer_num], precision=HIGHEST)
        right_gram = lax.dot_general(right_rows, right_rows, CONTRACT_ROWS, precision=HIGHEST)
        right_outs[layer_num] = right_new
        turned_outs[layer_num] = orthonormal(right_rows, right_gram, math.sqrt(channels))

    current = cotangent
    for layer_num in range(layer_total - 1, -1, -1):
        if layer_num > 0:
            extended = with_rims(jnp.stack([layer_inputs[layer_num], current]))
            backward = input_grad(extended[1], weights[layer_num - 1])
            following = (backward * silu_slope(preacts[layer_num - 1])).astype(jnp.bfloat16)
        else:
            extended = with_rims(layer_inputs[0][None])
            following = current
        gradient = weight_grad(extended[0], current)
        complete = lax.psum(gradient, ("dp", "space"))
        row_block = lax.dynamic_slice_in_dim(complete, space_index * row_share, row_share, 0)
        col_block = lax.dynamic_slice_in_dim(complete, dp_index * col_share, col_share, 0)
        gram_right = lax.dot_general(row_block, row_block, CONTRACT_ROWS, precision=HIGHEST)
        left_new = BETA * left_stats[layer_num] + (1.0 - BETA) * lax.dot_general(
            row_block, col_block, CONTRACT_COLS, precision=HIGHEST
        )
        left_outs[layer_num] = left_new
        product_rows = lax.psum(jnp.dot(left_new, left_basis[layer_num], precision=HIGHEST), "dp")
        gram_left = lax.dot_general(product_rows, product_rows, CONTRACT_ROWS, precision=HIGHEST)
        summed_left, summed_right = lax.psum((gram_left, gram_right), "space")
        finish(layer_num, product_rows, summed_left, summed_right)
        current = following
    return (
        jnp.stack(left_outs),
        jnp.stack(basis_outs),
        jnp.stack(right_outs),
        jnp.stack(turned_outs),
    )


def solution(mesh):
    placed = (
        P("dp", None, "space", None, None),
        P(None, "dp", None, "space", None, None),
        P("dp", None, "space", None, None),
        P(),
        P(None, "space", "dp"),
        P(None, "dp", None),
        P(),
        P(),
    )
    return jax.shard_map(
        local,
        mesh=mesh,
        in_specs=placed,
        out_specs=(P(None, "space", "dp"), P(), P(), P()),
        check_vma=False,
    )
```

profile of v0, /device:TPU:1, one launch (start us, length us, event | category | flops | bytes accessed | tf_op | source)
XLA Modules:
  0.0 1048.3 jit_solution(13744178759275144677)
XLA Ops:
  10.3 5.7 collective-permute-start.2
  25.9 4.0 reshape.307
  34.9 4.0 collective-permute-done.3
  41.2 5.5 pad_slice_fusion
  68.0 3.7 reshape.239
  74.8 4.1 reshape.240
  82.1 3.7 reshape.241
  95.7 3.7 reshape.243
  101.2 4.0 reshape.244
  118.8 3.8 convert_element_type.59
  153.1 4.3 concatenate.32
  157.4 4.9 concatenate.33
  164.2 161.1 %all-reduce.15.cloned.1.call-done = (f32[2880,320]{0,1:T(8,128)}, f32[2880,320]{0,1:T(8,128)}) async-done(((f32[2880,320]{0,1:T(8,128)}, f32[2880,320]{0,1:T(8,128)}), (f32[2880,320]{0,1:T(8,128)}, f32[2880,320]{0,1:T(8,128)})) %all-reduce.15.cloned.1.call-update) | async-done | bytes 7372816 | tf_op jit(solution)/shard_map/psum | solution.py:134
  340.3 108.4 %all-reduce.17.cloned.1.call-done = (f32[360,320]{0,1:T(8,128)}, f32[360,320]{0,1:T(8,128)}) async-done(((f32[360,320]{0,1:T(8,128)}, f32[360,320]{0,1:T(8,128)}), (f32[360,320]{0,1:T(8,128)}, f32[360,320]{0,1:T(8,128)})) %all-reduce.17.cloned.1.call-update) | async-done | bytes 921616 | tf_op jit(solution)/shard_map/psum | solution.py:142
  455.0 108.0 %all-reduce.19.cloned.1.call-done = (f32[320,320]{0,1:T(8,128)}, f32[320,320]{0,1:T(8,128)}, f32[320,320]{1,0:T(8,128)}, f32[320,320]{1,0:T(8,128)}) async-done(((f32[320,320]{0,1:T(8,128)}, f32[320,320]{0,1:T(8,128)}, f32[320,320]{1,0:T(8,128)}, f32[320,320]{1,0:T(8,128)}), (f32[320,320]{0,1:T(8,128)}, f32[320,320]{0,1:T(8,128)}, f32[320,320]{1,0:T(8,128)}, ...) | async-done | bytes 1638416 | tf_op jit(solution)/shard_map/psum | solution.py:144
  565.5 11.7 %cholesky.352 = f32[128,128]{1,0:T(8,128)S(1)} custom-call(f32[128,128]{1,0:T(8,128)S(1)} %cholesky.576), custom_call_target="Cholesky" | custom-call | tf_op jit(solution)/shard_map/jit(cholesky)/cholesky | solution.py:92
  577.3 9.8 custom-call.28
  589.4 11.7 %cholesky.371 = f32[128,128]{1,0:T(8,128)S(1)} custom-call(f32[128,128]{1,0:T(8,128)S(1)} %cholesky.580), custom_call_target="Cholesky" | custom-call | tf_op jit(solution)/shard_map/jit(cholesky)/cholesky | solution.py:92
  602.5 10.0 custom-call.29
  613.6 5.8 cholesky.393
  626.9 11.7 %cholesky.523 = f32[128,128]{1,0:T(8,128)S(1)} custom-call(f32[128,128]{1,0:T(8,128)S(1)} %cholesky.600), custom_call_target="Cholesky" | custom-call | tf_op jit(solution)/shard_map/jit(cholesky)/cholesky | solution.py:92
  638.7 9.8 custom-call.37
  650.8 12.1 %cholesky.542 = f32[128,128]{1,0:T(8,128)S(1)} custom-call(f32[128,128]{1,0:T(8,128)S(1)} %cholesky.604), custom_call_target="Cholesky" | custom-call | tf_op jit(solution)/shard_map/jit(cholesky)/cholesky | solution.py:92
  663.0 9.8 custom-call.38
  674.0 5.8 cholesky.564
  684.6 11.7 %cholesky.409 = f32[128,128]{1,0:T(8,128)S(1)} custom-call(f32[128,128]{1,0:T(8,128)S(1)} %cholesky.584), custom_call_target="Cholesky" | custom-call | tf_op jit(solution)/shard_map/jit(cholesky)/cholesky | solution.py:92
  698.5 11.4 %custom-call.31 = f32[1,128,128]{1,2,0:T(8,128)} custom-call(f32[1,128,128]{2,1,0:T(8,128)} %get-tuple-element.147), custom_call_target="InvertDiagBlocksLowerTriangular" | custom-call | tf_op jit(solution)/shard_map/jit(cholesky)/cholesky | solution.py:92
  713.5 13.2 %cholesky.428 = f32[128,128]{1,0:T(8,128)} custom-call(f32[128,128]{1,0:T(8,128)} %cholesky.588), custom_call_target="Cholesky" | custom-call | tf_op jit(solution)/shard_map/jit(cholesky)/cholesky | solution.py:92
  729.5 11.3 %custom-call.32 = f32[1,128,128]{1,2,0:T(8,128)} custom-call(f32[1,128,128]{2,1,0:T(8,128)} %get-tuple-element.144), custom_call_target="InvertDiagBlocksLowerTriangular" | custom-call | tf_op jit(solution)/shard_map/jit(cholesky)/cholesky | solution.py:92
  743.4 7.2 cholesky.450
  761.3 12.1 %cholesky.466 = f32[128,128]{1,0:T(8,128)S(1)} custom-call(f32[128,128]{1,0:T(8,128)S(1)} %cholesky.592), custom_call_target="Cholesky" | custom-call | tf_op jit(solution)/shard_map/jit(cholesky)/cholesky | solution.py:92
  775.5 11.3 %custom-call.34 = f32[1,128,128]{1,2,0:T(8,128)} custom-call(f32[1,128,128]{2,1,0:T(8,128)} %get-tuple-element.132), custom_call_target="InvertDiagBlocksLowerTriangular" | custom-call | tf_op jit(solution)/shard_map/jit(cholesky)/cholesky | solution.py:92
  790.4 13.2 %cholesky.485 = f32[128,128]{1,0:T(8,128)} custom-call(f32[128,128]{1,0:T(8,128)} %cholesky.596), custom_call_target="Cholesky" | custom-call | tf_op jit(solution)/shard_map/jit(cholesky)/cholesky | solution.py:92
  805.1 11.3 %custom-call.35 = f32[1,128,128]{1,2,0:T(8,128)} custom-call(f32[1,128,128]{2,1,0:T(8,128)} %get-tuple-element.129), custom_call_target="InvertDiagBlocksLowerTriangular" | custom-call | tf_op jit(solution)/shard_map/jit(cholesky)/cholesky | solution.py:92
  819.0 7.4 cholesky.507
  834.2 6.8 while.8
  844.2 30.9 %custom-call.30 = f32[3,128,128]{1,2,0:T(8,128)} custom-call(f32[3,128,128]{2,1,0:T(8,128)} %pad_maximum_fusion.7), custom_call_target="InvertDiagBlocksLowerTriangular" | custom-call | tf_op jit(solution)/shard_map/jit(_solve_triangular)/triangular_solve | solution.py:93
  884.6 5.9 while.9
  890.6 30.1 %custom-call.33 = f32[3,128,128]{1,2,0:T(8,128)} custom-call(f32[3,128,128]{2,1,0:T(8,128)S(1)} %pad_maximum_fusion.8), custom_call_target="InvertDiagBlocksLowerTriangular" | custom-call | tf_op jit(solution)/shard_map/jit(_solve_triangular)/triangular_solve | solution.py:93
  931.4 5.9 while.10
  937.3 29.5 %custom-call.36 = f32[3,128,128]{1,2,0:T(8,128)S(1)} custom-call(f32[3,128,128]{2,1,0:T(8,128)S(1)} %pad_maximum_fusion.9), custom_call_target="InvertDiagBlocksLowerTriangular" | custom-call | tf_op jit(solution)/shard_map/jit(_solve_triangular)/triangular_solve | solution.py:93
  966.9 5.8 while.11
  972.7 29.7 %custom-call.39 = f32[3,128,128]{1,2,0:T(8,128)S(1)} custom-call(f32[3,128,128]{2,1,0:T(8,128)S(1)} %pad_maximum_fusion.10), custom_call_target="InvertDiagBlocksLowerTriangular" | custom-call | tf_op jit(solution)/shard_map/jit(_solve_triangular)/triangular_solve | solution.py:93
  1011.7 6.3 copy.140
  1018.1 5.1 stack.48
  1023.1 6.3 copy.147
  1029.4 5.1 stack.49
  1034.5 6.8 pad_maximum_fusion
  (308 shorter events, 238.3 us)
Async XLA Ops:
  7.2 2.2 copy-start
  7.2 318.2 %all-reduce.15.cloned.1.call-start = ((), (), s32[]{:S(2)}) async-start(), calls=%async_computation.2 | async-start | bytes 15073280 | tf_op jit(solution)/shard_map/psum | solution.py:134
  9.4 14.3 %copy-start.2 = (bf16[1,1,1,8,240,320]{4,5,3,2,1,0:T(8,128)(2,1)S(1)}, bf16[1,1,1,8,240,320]{4,5,3,2,1,0:T(8,128)(2,1)}, u32[]{:S(2)}) copy-start(bf16[1,1,1,8,240,320]{4,5,3,2,1,0:T(8,128)(2,1)} %param.14) | copy-start | bytes 3686404
  10.3 24.5 %collective-permute-start.2 = (bf16[2,1,1,1,240,320]{4,5,3,2,1,0:T(8,128)(2,1)}, bf16[2,1,1,1,240,320]{4,5,3,2,1,0:T(8,128)(2,1)S(1)}, u32[]{:S(2)}, u32[]{:S(2)}) collective-permute-start(bf16[2,1,1,1,240,320]{4,5,3,2,1,0:T(8,128)(2,1)} %get-tuple-element.105), channel_id=1, source_target_pairs={{0,1},{1,2},{2,3},{3,4},{4,5},{5,6},{6,7},{8,9},{9,10},{10,11},{11... | collective-permute-start | bytes 921608 | tf_op jit(solution)/shard_map/ppermute | solution.py:22
  17.7 12.2 %collective-permute-start = (bf16[1,1,1,1,240,320]{4,5,3,2,1,0:T(8,128)(2,1)}, bf16[1,1,1,1,240,320]{4,5,3,2,1,0:T(8,128)(2,1)S(1)}, u32[]{:S(2)}, u32[]{:S(2)}) collective-permute-start(bf16[1,1,1,1,240,320]{4,5,3,2,1,0:T(8,128)(2,1)} %get-tuple-element.116), channel_id=1, source_target_pairs={{0,1},{1,2},{2,3},{3,4},{4,5},{5,6},{6,7},{8,9},{9,10},{10,11},{11... | collective-permute-start | bytes 460808 | tf_op jit(solution)/shard_map/ppermute | solution.py:22
  21.0 10.9 %collective-permute-start.1 = (bf16[1,1,1,1,240,320]{4,5,3,2,1,0:T(8,128)(2,1)}, bf16[1,1,1,1,240,320]{4,5,3,2,1,0:T(8,128)(2,1)}, u32[]{:S(2)}, u32[]{:S(2)}) collective-permute-start(bf16[1,1,1,1,240,320]{4,5,3,2,1,0:T(8,128)(2,1)} %get-tuple-element.117), channel_id=1, source_target_pairs={{1,0},{2,1},{3,2},{4,3},{5,4},{6,5},{7,6},{9,8},{10,9},{11,10},{12... | collective-permute-start | bytes 460808 | tf_op jit(solution)/shard_map/ppermute | solution.py:23
  22.3 16.5 %collective-permute-start.3 = (bf16[2,1,1,1,240,320]{4,5,3,2,1,0:T(8,128)(2,1)}, bf16[2,1,1,1,240,320]{4,5,3,2,1,0:T(8,128)(2,1)S(1)}, u32[]{:S(2)}, u32[]{:S(2)}) collective-permute-start(bf16[2,1,1,1,240,320]{4,5,3,2,1,0:T(8,128)(2,1)} %get-tuple-element.106), channel_id=1, source_target_pairs={{1,0},{2,1},{3,2},{4,3},{5,4},{6,5},{7,6},{9,8},{10,9},{11,10},{12... | collective-permute-start | bytes 921608 | tf_op jit(solution)/shard_map/ppermute | solution.py:23
  101.2 4.0 copy-start.15
  105.2 1.3 copy-start.3
  106.5 1.3 copy-start.4
  107.8 1.3 copy-start.5
  109.1 1.3 copy-start.6
  110.3 1.3 copy-start.7
  111.6 1.3 copy-start.8
  112.9 1.3 copy-start.9
  114.2 1.7 copy-start.13
  114.2 2.0 copy-start.31
  118.8 3.8 copy-start.26
  135.5 1.7 copy-start.1
  135.5 1.8 copy-start.27
  151.3 1.8 copy-start.35
  151.3 1.8 copy-start.36
  151.3 1.8 copy-start.37
  151.3 1.8 copy-start.38
  151.3 1.8 copy-start.39
  151.3 1.8 copy-start.40
  162.3 1.1 copy-start.33
  162.3 1.5 copy-start.34
  162.3 286.3 %all-reduce.17.cloned.1.call-start = ((), (), s32[]{:S(2)}) async-start(), calls=%async_computation.3 | async-start | bytes 1966080 | tf_op jit(solution)/shard_map/psum | solution.py:142
  333.5 229.5 %all-reduce.19.cloned.1.call-start = ((), (), s32[]{:S(2)}) async-start(), calls=%async_computation.4 | async-start | bytes 3932160 | tf_op jit(solution)/shard_map/psum | solution.py:144
  448.7 3.1 copy-start.10
  453.6 558.1 %all-gather.5.cloned.1.call-start = ((), (), s32[]{:S(2)}) async-start(), calls=%async_computation | async-start | bytes 4423680 | tf_op jit(solution)/shard_map/all_gather | solution.py:117
  563.0 1.3 copy-start.20
  563.0 1.6 copy-start.21
  565.5 11.8 %copy-start.28 = (f32[320,320]{1,0:T(8,128)}, f32[320,320]{1,0:T(8,128)S(1)}, u32[]{:S(2)}) copy-start(f32[320,320]{1,0:T(8,128)S(1)} %get-tuple-element.165) | copy-start | bytes 1228804
  577.3 45.7 %copy-start.12 = (f32[2,320,320]{2,1,0:T(8,128)S(1)}, f32[2,320,320]{2,1,0:T(8,128)}, u32[]{:S(2)}) copy-start(f32[2,320,320]{2,1,0:T(8,128)} %param.19) | copy-start | bytes 2457604
  577.3 45.7 %copy-start.22 = (f32[320,320]{1,0:T(8,128)S(1)}, f32[320,320]{1,0:T(8,128)}, u32[]{:S(2)}) copy-start(f32[320,320]{1,0:T(8,128)} %get-tuple-element.93) | copy-start | bytes 1228804
  622.1 1.4 copy-start.32
  683.2 70.8 %copy-start.16 = (f32[320,320]{1,0:T(8,128)}, f32[320,320]{1,0:T(8,128)S(1)}, u32[]{:S(2)}) copy-start(f32[320,320]{1,0:T(8,128)S(1)} %select_select_fusion) | copy-start | bytes 1228804
  753.9 1.2 copy-start.24
  827.1 3.1 copy-start.14
  830.3 44.8 %copy-start.11 = (f32[360,320]{0,1:T(8,128)S(1)}, f32[360,320]{0,1:T(8,128)}, u32[]{:S(2)}) copy-start(f32[360,320]{0,1:T(8,128)} %get-tuple-element.90) | copy-start | bytes 1382404
  882.5 8.1 copy-start.47
  884.6 138.6 %all-gather.7.cloned.1.call-start = ((), (), s32[]{:S(2)}) async-start(), calls=%async_computation.1 | async-start | bytes 4423680 | tf_op jit(solution)/shard_map/all_gather | solution.py:117
  930.3 7.0 copy-start.46
  931.4 41.3 %copy-start.45 = (f32[1,128,128]{2,1,0:T(8,128)S(1)}, f32[1,128,128]{2,1,0:T(8,128)}, u32[]{:S(2)}) copy-start(f32[1,128,128]{2,1,0:T(8,128)} %get-tuple-element.126) | copy-start | bytes 196612
  1009.1 1.1 copy-start.23
  1009.1 1.5 copy-start.25
  (9 other events, 6.5 us)
Sparse Core Ops, SparseCore 0:
  162.5 162.8 all-reduce.14
  333.6 115.0 all-reduce.16
  453.8 109.2 all-reduce.18
  884.7 68.0 all-gather.4
  955.0 67.3 all-gather.6
where the time goes:
time: 1060 us; the launch traced here: 1050 us
  waiting for transfers between devices  384 us (36%)
  other arithmetic  367 us (35%)
  local copies, waits for them, and re-layouts  161 us (15%)
  matrix products  102 us (10%)
  between operations  22.8 us (2%)
  starting transfers between devices  11.9 us (1%)
    another operation x42, other arithmetic, orthonormal(): lower_factor = jnp.linalg.cholesky(gram_matrix)  221 us
    psum x1, waiting for transfers between devices, local(): complete = lax.psum(gradient, ('dp', 'space'))  161 us
    another operation x16, other arithmetic, orthonormal(): jax.scipy.linalg.solve_triangular(lower_factor, product_rows.T, lower=True)  126 us
    psum x1, waiting for transfers between devices, local(): lax.psum(jnp.dot(left_new, left_basis[layer_num], precision=HIGHEST), 'dp')  108 us
    psum x1, waiting for transfers between devices, local(): summed_left, summed_right = lax.psum((gram_left, gram_right), 'space')  108 us
    reshape x9, local copies, waits for them, and re-layouts, input_grad(): shifted.reshape(-1, channels)  32.9 us
    slice x10, local copies, waits for them, and re-layouts, input_grad(): padded[:, :, 1 - row_step:1 - row_step + row_count, 1 - col_step:1 - col_...  31.1 us
    dot_general x18, matrix products, weight_grad(): lax.dot_general(shifted.reshape(-1, channels), flat_grad, CONTRACT_ROWS,...  30.3 us
  transfers between devices with their start and end apart: 9, of which 5 were waited for; matrix products, arithmetic and copies ran while one was open for 15% of the time, Pallas kernels for 0%

commit v1 on v0

--- a/solution.py
+++ b/solution.py
@@ -3,6 +3,8 @@
 import jax
 import jax.numpy as jnp
 from jax import lax
+from jax.experimental import pallas as pl
+from jax.experimental.pallas import tpu as pltpu
 from jax.sharding import PartitionSpec as P
 
 BETA = 0.95
@@ -88,10 +90,71 @@
     return summed.reshape(grad_rims.shape[0], grad_rims.shape[1], row_count, col_count, channels)
 
 
-def orthonormal(product_rows, gram_matrix, factor):
-    lower_factor = jnp.linalg.cholesky(gram_matrix)
-    solved = jax.scipy.linalg.solve_triangular(lower_factor, product_rows.T, lower=True)
-    return solved.T * factor
+NB = 64
+
+def diag_inverse(blocks):
+    n = NB
+    row = lax.broadcasted_iota(jnp.int32, (n, 2 * n), 0)
+    col = lax.broadcasted_iota(jnp.int32, (n, 2 * n), 1)
+    eye = jnp.where(row + n == col, 1.0, 0.0).astype(jnp.float32)
+    tiles = []
+    for b in blocks:
+        x = jnp.concatenate([b, jnp.zeros((n, n), jnp.float32)], axis=1) + eye
+        tiles.append([x[8 * t:8 * t + 8] for t in range(n // 8)])
+    sub = lax.broadcasted_iota(jnp.int32, (8, 2 * n), 0)
+    scales = [[None] * (n // 8) for _ in blocks]
+    for j in range(n):
+        tj, sj = j // 8, j % 8
+        for m in range(len(blocks)):
+            x = tiles[m]
+            pivot_row = x[tj][sj:sj + 1, :]
+            cb = jnp.broadcast_to(x[tj][:, j:j + 1], (8, 2 * n))
+            d = cb[sj:sj + 1, :]
+            rs = lax.rsqrt(d)
+            scales[m][tj] = jnp.where(sub == sj, rs, scales[m][tj] if sj else 0.0)
+            scaled = pivot_row * (rs * rs)
+            if sj < 7:
+                x[tj] = x[tj] - jnp.where(sub > sj, cb, 0.0) * scaled
+            for t in range(tj + 1, n // 8):
+                x[t] = x[t] - jnp.broadcast_to(x[t][:, j:j + 1], (8, 2 * n)) * scaled
+    out = []
+    for m in range(len(blocks)):
+        w = jnp.concatenate([tiles[m][t] * scales[m][t] for t in range(n // 8)], axis=0)
+        out.append(w[:, n:])
+    return out
+
+def chol_inv_kernel(g_ref, o_ref):
+    nm, size, _ = g_ref.shape
+    o_ref[...] = g_ref[...]
+    nblk = size // NB
+    for k in range(nblk):
+        o = k * NB
+        linv = diag_inverse([o_ref[m, o:o + NB, o:o + NB] for m in range(nm)])
+        for m in range(nm):
+            parts = []
+            prow = o_ref[m, o:o + NB, :]
+            r = jnp.dot(linv[m], prow, precision=HIGHEST, preferred_element_type=jnp.float32)
+            pieces = []
+            if k: pieces.append(r[:, :o])
+            pieces.append(linv[m])
+            if k < nblk - 1: pieces.append(r[:, o + NB:])
+            rz = jnp.concatenate(pieces, axis=1)
+            if k < nblk - 1:
+                below = r[:, o + NB:]
+                upd = lax.dot_general(below, rz, (((0,), (0,)), ((), ())), precision=HIGHEST, preferred_element_type=jnp.float32)
+                old = o_ref[m, o + NB:, :]
+                colid = lax.broadcasted_iota(jnp.int32, old.shape, 1)
+                old = jnp.where((colid >= o) & (colid < o + NB), 0.0, old)
+                o_ref[m, o + NB:, :] = old - upd
+                colr = lax.broadcasted_iota(jnp.int32, rz.shape, 1)
+                o_ref[m, o:o + NB, :] = jnp.where(colr < o + NB, rz, 0.0)
+            else:
+                o_ref[m, o:o + NB, :] = rz
+
+def chol_inv(grams):
+    return pl.pallas_call(chol_inv_kernel, out_shape=jax.ShapeDtypeStruct(grams.shape, jnp.float32),
+        in_specs=[pl.BlockSpec(memory_space=pltpu.VMEM)], out_specs=pl.BlockSpec(memory_space=pltpu.VMEM),
+        compiler_params=pltpu.CompilerParams(vmem_limit_bytes=48*1024*1024))(grams)
 
 
 def with_rims(stacked):
@@ -112,15 +175,7 @@
     right_outs = [None] * layer_total
     turned_outs = [None] * layer_total
 
-    def finish(layer_num, product_rows, gram_left, gram_right):
-        basis_rows = orthonormal(product_rows, gram_left, math.sqrt(full_rows))
-        basis_outs[layer_num] = lax.all_gather(basis_rows, "space", axis=0, tiled=True)
-        right_new = BETA * right_stats[layer_num] + (1.0 - BETA) * gram_right
-        right_rows = jnp.dot(right_new, right_basis[layer_num], precision=HIGHEST)
-        right_gram = lax.dot_general(right_rows, right_rows, CONTRACT_ROWS, precision=HIGHEST)
-        right_outs[layer_num] = right_new
-        turned_outs[layer_num] = orthonormal(right_rows, right_gram, math.sqrt(channels))
-
+    pieces = [None] * layer_total
     current = cotangent
     for layer_num in range(layer_total - 1, -1, -1):
         if layer_num > 0:
@@ -142,8 +197,23 @@
         product_rows = lax.psum(jnp.dot(left_new, left_basis[layer_num], precision=HIGHEST), "dp")
         gram_left = lax.dot_general(product_rows, product_rows, CONTRACT_ROWS, precision=HIGHEST)
         summed_left, summed_right = lax.psum((gram_left, gram_right), "space")
-        finish(layer_num, product_rows, summed_left, summed_right)
+        right_new = BETA * right_stats[layer_num] + (1.0 - BETA) * summed_right
+        right_rows = jnp.dot(right_new, right_basis[layer_num], precision=HIGHEST)
+        right_gram = lax.dot_general(right_rows, right_rows, CONTRACT_ROWS, precision=HIGHEST)
+        right_outs[layer_num] = right_new
+        pieces[layer_num] = (product_rows, summed_left, right_rows, right_gram)
         current = following
+    inverses = chol_inv(
+        jnp.stack([p[1] for p in pieces] + [p[3] for p in pieces])
+    )
+    for i in range(layer_total):
+        rows = math.sqrt(full_rows) * lax.dot_general(
+            pieces[i][0], inverses[i], CONTRACT_COLS, precision=HIGHEST
+        )
+        basis_outs[i] = lax.all_gather(rows, "space", axis=0, tiled=True)
+        turned_outs[i] = math.sqrt(channels) * lax.dot_general(
+            pieces[i][2], inverses[layer_total + i], CONTRACT_COLS, precision=HIGHEST
+        )
     return (
         jnp.stack(left_outs),
         jnp.stack(basis_outs),

time: 1060 us -> 782 us (0.74)
  other arithmetic: 367 us -> 16.5 us
  waiting for transfers between devices: 384 us -> 502 us
  local copies, waits for them, and re-layouts: 161 us -> 117 us
  Pallas kernels: 0 us -> 36.5 us
  matrix products: 102 us -> 71.5 us
    another operation x61 -> x1, other arithmetic: 348 us -> 0.13 us  [local(): jnp.stack([p[1] for p in pieces] + [p[3] for p in pieces])]
    all_gather x2, waiting for transfers between devices: 0.01 us -> 118 us  [local(): basis_outs[i] = lax.all_gather(rows, 'space', axis=0, tiled=True)]
    pallas_call x0 -> x1, Pallas kernels: none -> 36.5 us  [chol_inv(): pl.pallas_call(chol_inv_kernel, out_shape=jax.ShapeDtypeStruct(grams.shap...]
    another operation x36 -> x0, matrix products: 36.1 us -> none  [the longest x20 19.4 us: orthonormal(): jax.scipy.linalg.solve_triangular(lower_factor, product_rows.T, lower=True)]
    another operation x45 -> x0, local copies, waits for them, and re-layouts: 31.5 us -> none  [the longest x33 27.5 us: orthonormal(): jax.scipy.linalg.solve_triangular(lower_factor, product_rows.T, lower=True)]
  transfers between devices with their start and end apart: 9 -> 9, of which waited for: 5 -> 7; matrix products, arithmetic and copies ran while one was open for 15% -> 5% of each run, Pallas kernels for 0% -> 0%
where the time goes in v1:
time: 782 us; the launch traced here: 771 us
  waiting for transfers between devices  502 us (64%)
  local copies, waits for them, and re-layouts  117 us (15%)
  matrix products  71.5 us (9%)
  Pallas kernels  36.5 us (5%)
  other arithmetic  16.5 us (2%)
  between operations  14.7 us (2%)
  starting transfers between devices  12.1 us (2%)
    psum x1, waiting for transfers between devices, local(): complete = lax.psum(gradient, ('dp', 'space'))  161 us
    all_gather x2, waiting for transfers between devices, local(): basis_outs[i] = lax.all_gather(rows, 'space', axis=0, tiled=True)  118 us
    psum x1, waiting for transfers between devices, local(): summed_left, summed_right = lax.psum((gram_left, gram_right), 'space')  109 us
    psum x1, waiting for transfers between devices, local(): lax.psum(jnp.dot(left_new, left_basis[layer_num], precision=HIGHEST), 'dp')  108 us
    pallas_call x1, Pallas kernels, chol_inv(): pl.pallas_call(chol_inv_kernel, out_shape=jax.ShapeDtypeStruct(grams.shap...  36.5 us
    reshape x9, local copies, waits for them, and re-layouts, input_grad(): shifted.reshape(-1, channels)  32.8 us
    slice x10, local copies, waits for them, and re-layouts, input_grad(): padded[:, :, 1 - row_step:1 - row_step + row_count, 1 - col_step:1 - col_...  31.1 us
    dot_general x18, matrix products, weight_grad(): lax.dot_general(shifted.reshape(-1, channels), flat_grad, CONTRACT_ROWS,...  30.1 us
  transfers between devices with their start and end apart: 9, of which 7 were waited for; matrix products, arithmetic and copies ran while one was open for 5% of the time, Pallas kernels for 0%

profile of v1, /device:TPU:1, one launch (start us, length us, event | category | flops | bytes accessed | tf_op | source)
XLA Modules:
  0.0 770.8 jit_solution(12685869035294288575)
XLA Ops:
  7.2 2.1 multiply_convert_fusion
  10.3 5.7 collective-permute-start.2
  17.7 3.3 collective-permute-start
  23.6 2.3 copy.61
  25.9 4.0 reshape.230
  29.9 2.1 collective-permute-done.1
  32.0 2.9 maximum_bitcast_fusion
  34.9 4.0 collective-permute-done.3
  41.2 5.5 pad_slice_fusion
  48.6 2.8 reshape.203
  51.4 3.1 copy.53
  54.5 3.7 reshape.204
  58.1 3.1 copy.54
  61.3 3.7 reshape.205
  64.9 3.1 copy.55
  68.1 3.7 reshape.206
  71.7 3.1 copy.56
  74.8 3.8 reshape.207
  78.7 3.1 copy.57
  81.8 3.7 reshape.208
  85.5 3.2 copy.58
  88.7 3.7 reshape.209
  92.3 3.1 copy.59
  95.4 3.7 reshape.210
  100.9 4.2 reshape.211
  116.2 2.6 fusion.1
  118.8 3.7 convert_element_type.59
  149.1 2.0 fusion.91
  152.8 4.3 concatenate.14
  157.1 4.9 concatenate.15
  164.0 161.3 %all-reduce.10.cloned.1.call-done = (f32[2880,320]{0,1:T(8,128)}, f32[2880,320]{0,1:T(8,128)}) async-done(((f32[2880,320]{0,1:T(8,128)}, f32[2880,320]{0,1:T(8,128)}), (f32[2880,320]{0,1:T(8,128)}, f32[2880,320]{0,1:T(8,128)})) %all-reduce.10.cloned.1.call-update) | async-done | bytes 7372816 | tf_op jit(solution)/shard_map/psum | solution.py:189
  325.3 2.4 fusion.117
  330.0 2.4 fusion.118
  334.8 3.4 fusion.137
  338.3 3.3 fusion.140
  341.6 108.2 %all-reduce.12.cloned.1.call-done = (f32[360,320]{0,1:T(8,128)}, f32[360,320]{0,1:T(8,128)}) async-done(((f32[360,320]{0,1:T(8,128)}, f32[360,320]{0,1:T(8,128)}), (f32[360,320]{0,1:T(8,128)}, f32[360,320]{0,1:T(8,128)})) %all-reduce.12.cloned.1.call-update) | async-done | bytes 921616 | tf_op jit(solution)/shard_map/psum | solution.py:197
  449.7 3.1 convolution_bitcast_fusion.2
  455.2 108.9 %all-reduce.14.cloned.1.call-done = (f32[320,320]{1,0:T(8,128)}, f32[320,320]{1,0:T(8,128)}, f32[1,320,320]{2,1,0:T(8,128)}, f32[1,320,320]{2,1,0:T(8,128)}) async-done(((f32[320,320]{1,0:T(8,128)}, f32[320,320]{1,0:T(8,128)}, f32[1,320,320]{2,1,0:T(8,128)}, f32[1,320,320]{2,1,0:T(8,128)}), (f32[320,320]{1,0:T(8,128)}, f32[320,320]{1,0:T(8,128)}, f32[1,320,320]{2,1,0:T(8,128)}, ...) | async-done | bytes 1638416 | tf_op jit(solution)/shard_map/psum | solution.py:199
  564.1 2.3 fusion.131
  570.2 36.5 %shard_map.111 = f32[4,320,320]{2,1,0:T(8,128)S(1)} custom-call(f32[4,320,320]{2,1,0:T(8,128)S(1)} %pad_maximum_fusion.2.g_ref), custom_call_target="tpu_custom_call" | custom-call | tf_op jit(solution)/shard_map/pallas_call | solution.py:155
  608.7 1.9 fusion.115
  616.6 59.7 %all-gather.5.cloned.1.call-done = f32[8,360,320]{1,2,0:T(8,128)} async-done(((f32[1,360,320]{1,2,0:T(8,128)}), f32[8,360,320]{1,2,0:T(8,128)}) %all-gather.5.cloned.1.call-update) | async-done | bytes 3686416 | tf_op jit(solution)/shard_map/all_gather | solution.py:213
  676.3 6.3 copy.74
  682.6 5.1 stack.68
  687.8 57.9 %all-gather.7.cloned.1.call-done = f32[8,360,320]{1,2,0:T(8,128)} async-done(((f32[1,360,320]{1,2,0:T(8,128)}), f32[8,360,320]{1,2,0:T(8,128)}) %all-gather.7.cloned.1.call-update) | async-done | bytes 3686416 | tf_op jit(solution)/shard_map/all_gather | solution.py:213
  745.6 6.3 copy.75
  752.0 5.1 stack.69
  757.1 6.8 pad_maximum_fusion
  (135 shorter events, 71.1 us)
Async XLA Ops:
  7.2 2.2 copy-start
  7.2 318.1 %all-reduce.10.cloned.1.call-start = ((), (), s32[]{:S(2)}) async-start(), calls=%async_computation.2 | async-start | bytes 15073280 | tf_op jit(solution)/shard_map/psum | solution.py:189
  9.4 14.3 %copy-start.2 = (bf16[1,1,1,8,240,320]{4,5,3,2,1,0:T(8,128)(2,1)S(1)}, bf16[1,1,1,8,240,320]{4,5,3,2,1,0:T(8,128)(2,1)}, u32[]{:S(2)}) copy-start(bf16[1,1,1,8,240,320]{4,5,3,2,1,0:T(8,128)(2,1)} %param.9) | copy-start | bytes 3686404
  10.3 24.6 %collective-permute-start.2 = (bf16[2,1,1,1,240,320]{4,5,3,2,1,0:T(8,128)(2,1)}, bf16[2,1,1,1,240,320]{4,5,3,2,1,0:T(8,128)(2,1)S(1)}, u32[]{:S(2)}, u32[]{:S(2)}) collective-permute-start(bf16[2,1,1,1,240,320]{4,5,3,2,1,0:T(8,128)(2,1)} %get-tuple-element.26), channel_id=1, source_target_pairs={{0,1},{1,2},{2,3},{3,4},{4,5},{5,6},{6,7},{8,9},{9,10},{10,11},{11... | collective-permute-start | bytes 921608 | tf_op jit(solution)/shard_map/ppermute | solution.py:24
  17.7 12.2 %collective-permute-start = (bf16[1,1,1,1,240,320]{4,5,3,2,1,0:T(8,128)(2,1)}, bf16[1,1,1,1,240,320]{4,5,3,2,1,0:T(8,128)(2,1)S(1)}, u32[]{:S(2)}, u32[]{:S(2)}) collective-permute-start(bf16[1,1,1,1,240,320]{4,5,3,2,1,0:T(8,128)(2,1)} %get-tuple-element.37), channel_id=1, source_target_pairs={{0,1},{1,2},{2,3},{3,4},{4,5},{5,6},{6,7},{8,9},{9,10},{10,11},{11... | collective-permute-start | bytes 460808 | tf_op jit(solution)/shard_map/ppermute | solution.py:24
  21.0 11.0 %collective-permute-start.1 = (bf16[1,1,1,1,240,320]{4,5,3,2,1,0:T(8,128)(2,1)}, bf16[1,1,1,1,240,320]{4,5,3,2,1,0:T(8,128)(2,1)}, u32[]{:S(2)}, u32[]{:S(2)}) collective-permute-start(bf16[1,1,1,1,240,320]{4,5,3,2,1,0:T(8,128)(2,1)} %get-tuple-element.38), channel_id=1, source_target_pairs={{1,0},{2,1},{3,2},{4,3},{5,4},{6,5},{7,6},{9,8},{10,9},{11,10},{12... | collective-permute-start | bytes 460808 | tf_op jit(solution)/shard_map/ppermute | solution.py:25
  22.3 16.6 %collective-permute-start.3 = (bf16[2,1,1,1,240,320]{4,5,3,2,1,0:T(8,128)(2,1)}, bf16[2,1,1,1,240,320]{4,5,3,2,1,0:T(8,128)(2,1)S(1)}, u32[]{:S(2)}, u32[]{:S(2)}) collective-permute-start(bf16[2,1,1,1,240,320]{4,5,3,2,1,0:T(8,128)(2,1)} %get-tuple-element.27), channel_id=1, source_target_pairs={{1,0},{2,1},{3,2},{4,3},{5,4},{6,5},{7,6},{9,8},{10,9},{11,10},{12... | collective-permute-start | bytes 921608 | tf_op jit(solution)/shard_map/ppermute | solution.py:25
  100.9 4.2 copy-start.18
  105.1 1.3 copy-start.3
  106.4 1.3 copy-start.4
  107.7 1.3 copy-start.5
  109.0 1.3 copy-start.6
  110.3 1.3 copy-start.7
  111.6 1.3 copy-start.8
  112.8 1.3 copy-start.9
  114.1 1.7 copy-start.17
  114.1 2.0 copy-start.24
  118.8 3.7 copy-start.22
  135.4 1.7 copy-start.1
  135.4 1.8 copy-start.23
  151.0 1.8 copy-start.31
  151.0 1.8 copy-start.32
  151.0 1.8 copy-start.33
  151.0 1.8 copy-start.34
  151.0 1.8 copy-start.35
  151.1 1.8 copy-start.36
  162.0 1.1 copy-start.27
  162.0 1.5 copy-start.28
  162.1 287.7 %all-reduce.12.cloned.1.call-start = ((), (), s32[]{:S(2)}) async-start(), calls=%async_computation.3 | async-start | bytes 1966080 | tf_op jit(solution)/shard_map/psum | solution.py:197
  327.6 0.7 copy-start.15
  332.4 0.7 copy-start.16
  334.8 229.3 %all-reduce.14.cloned.1.call-start = ((), (), s32[]{:S(2)}) async-start(), calls=%async_computation.4 | async-start | bytes 3932160 | tf_op jit(solution)/shard_map/psum | solution.py:199
  449.7 3.1 copy-start.11
  452.8 111.3 %copy-start.13 = (f32[2,320,320]{2,1,0:T(8,128)S(1)}, f32[2,320,320]{2,1,0:T(8,128)}, u32[]{:S(2)}) copy-start(f32[2,320,320]{2,1,0:T(8,128)} %param.14) | copy-start | bytes 2457604
  452.8 111.3 %copy-start.25 = (f32[2,320,320]{2,1,0:T(8,128)S(1)}, f32[2,320,320]{2,1,0:T(8,128)}, u32[]{:S(2)}) copy-start(f32[2,320,320]{2,1,0:T(8,128)} %param.15) | copy-start | bytes 2457604
  454.7 221.6 %all-gather.5.cloned.1.call-start = ((), (), s32[]{:S(2)}) async-start(), calls=%async_computation | async-start | bytes 4423680 | tf_op jit(solution)/shard_map/all_gather | solution.py:213
  564.1 3.5 copy-start.20
  564.1 3.5 copy-start.26
  567.7 2.4 copy-start.29
  567.7 2.4 copy-start.30
  570.2 36.5 %copy-start.12 = (f32[360,320]{0,1:T(8,128)S(1)}, f32[360,320]{0,1:T(8,128)}, u32[]{:S(2)}) copy-start(f32[360,320]{0,1:T(8,128)} %get-tuple-element.19) | copy-start | bytes 1382404
  606.7 2.0 copy-start.10
  608.6 137.0 %all-gather.7.cloned.1.call-start = ((), (), s32[]{:S(2)}) async-start(), calls=%async_computation.1 | async-start | bytes 4423680 | tf_op jit(solution)/shard_map/all_gather | solution.py:213
  612.8 2.2 copy-start.14
  612.8 2.2 copy-start.19
  612.8 2.2 copy-start.21
Sparse Core Ops, SparseCore 0:
  162.2 163.0 all-reduce.9
  334.9 114.7 all-reduce.11
  454.8 109.2 all-reduce.13
  608.7 67.5 all-gather.4
  678.5 67.1 all-gather.6

commit v2 on v1

--- a/solution.py
+++ b/solution.py
@@ -1,3 +1,4 @@
+import functools
 import math
 
 import jax
@@ -157,69 +158,290 @@
         compiler_params=pltpu.CompilerParams(vmem_limit_bytes=48*1024*1024))(grams)
 
 
+def coords():
+    dp, space = lax.axis_index("dp"), lax.axis_index("space")
+    core, x, y = dp % 2, (dp // 2) % 4, (space % 2) * 2 + dp // 8
+    return core, (x, y, space // 2)
+
+def device_at(core, place):
+    x, y, z = place
+    return {"dp": ((y % 2) * 4 + x) * 2 + core, "space": z * 2 + y // 2}
+
+def shifted_place(place, axis, step):
+    moved = list(place)
+    moved[axis] = (place[axis] + step) % 4
+    return tuple(moved)
+
+def greet(partners):
+    barrier = pltpu.get_barrier_semaphore()
+    for partner in partners:
+        pl.semaphore_signal(barrier, inc=1, device_id=partner, device_id_type=pl.DeviceIdType.MESH)
+    pl.semaphore_wait(barrier, len(partners))
+
+def add_rows(dst, dst_row, terms, rows, step):
+    def body(i, carry):
+        total = None
+        for ref, start in terms:
+            first = pl.multiple_of(start + i * step, 8)
+            value = ref[pl.ds(first, step), :]
+            total = value if total is None else total + value
+        dst[pl.ds(pl.multiple_of(dst_row + i * step, 8), step), :] = total
+        return carry
+    lax.fori_loop(0, rows // step, body, 0)
+
+def reduce_kernel(g_ref, o_ref, r0, r1, b, r2, c, r3, f, send, recv):
+    core, place = coords()
+    orders = [(0, 1, 2), (1, 2, 0), (2, 0, 1)]
+    sibling = device_at(1 - core, place)
+    partners = [sibling]
+    for axis in range(3):
+        for step in (1, 2, 3):
+            partners.append(device_at(core, shifted_place(place, axis, step)))
+    greet(partners)
+    copies = []
+    def start(src, dst, to):
+        n = len(copies)
+        copy = pltpu.make_async_remote_copy(src_ref=src, dst_ref=dst, send_sem=send.at[n], recv_sem=recv.at[n],
+            device_id=to, device_id_type=pl.DeviceIdType.MESH)
+        copy.start()
+        copies.append(copy)
+        return copy
+    part = 960
+    first = [start(g_ref.at[1 - core, pl.ds(p * part, part)], r0.at[pl.ds(p * part, part)], sibling) for p in range(3)]
+    level1, level2, level3 = [], [], []
+    for p in range(3):
+        first[p].wait_recv()
+        add_rows(r0, p * part, [(r0, p * part), (g_ref.at[core], p * part)], part, 96)
+        axis = orders[p][0]
+        sends = []
+        for step in (1, 2, 3):
+            to = shifted_place(place, axis, step)
+            src = pl.multiple_of(p * part + to[axis] * 240, 8)
+            sends.append(start(r0.at[pl.ds(src, 240)], r1.at[p, step - 1], device_at(core, to)))
+        level1.append(sends)
+    for p in range(3):
+        for copy in level1[p]:
+            copy.wait_recv()
+        mine = place[orders[p][0]]
+        add_rows(b.at[p], 0, [(r0, p * part + mine * 240)] + [(r1.at[p, k], 0) for k in range(3)], 240, 48)
+        b[p, 240:, :] = jnp.zeros((16, b.shape[2]), jnp.float32)
+        axis = orders[p][1]
+        sends = []
+        for step in (1, 2, 3):
+            to = shifted_place(place, axis, step)
+            src = pl.multiple_of(to[axis] * 64, 8)
+            sends.append(start(b.at[p, pl.ds(src, 64)], r2.at[p, step - 1], device_at(core, to)))
+        level2.append(sends)
+    for p in range(3):
+        for copy in level2[p]:
+            copy.wait_recv()
+        mine = place[orders[p][1]]
+        add_rows(c.at[p], 0, [(b.at[p], mine * 64)] + [(r2.at[p, k], 0) for k in range(3)], 64, 64)
+        axis = orders[p][2]
+        sends = []
+        for step in (1, 2, 3):
+            to = shifted_place(place, axis, step)
+            src = pl.multiple_of(to[axis] * 16, 8)
+            sends.append(start(c.at[p, pl.ds(src, 16)], r3.at[p, step - 1], device_at(core, to)))
+        level3.append(sends)
+    gather3, gather2, gather1, last = [], [], [], []
+    for p in range(3):
+        for copy in level3[p]:
+            copy.wait_recv()
+        axis = orders[p][2]
+        row = pl.multiple_of(place[orders[p][1]] * 64 + place[axis] * 16, 8)
+        add_rows(f.at[p], row, [(c.at[p], place[axis] * 16)] + [(r3.at[p, k], 0) for k in range(3)], 16, 16)
+        here = f.at[p, pl.ds(row, 16)]
+        gather3.append([start(here, here, device_at(core, shifted_place(place, axis, s))) for s in (1, 2, 3)])
+    for p in range(3):
+        for copy in gather3[p]:
+            copy.wait_recv()
+        axis = orders[p][1]
+        here = f.at[p, pl.ds(pl.multiple_of(place[axis] * 64, 8), 64)]
+        gather2.append([start(here, here, device_at(core, shifted_place(place, axis, s))) for s in (1, 2, 3)])
+    for p in range(3):
+        for copy in gather2[p]:
+            copy.wait_recv()
+        axis = orders[p][0]
+        row = pl.multiple_of(p * part + place[axis] * 240, 8)
+        src = f.at[p, pl.ds(0, 240)]
+        gather1.append([start(src, o_ref.at[core, pl.ds(row, 240)], device_at(core, shifted_place(place, axis, s)))
+                        for s in (1, 2, 3)])
+        add_rows(o_ref.at[core], row, [(f.at[p], 0)], 240, 48)
+    for p in range(3):
+        for copy in gather1[p]:
+            copy.wait_recv()
+        here = o_ref.at[core, pl.ds(p * part, part)]
+        last.append(start(here, here, sibling))
+    for copy in last:
+        copy.wait_recv()
+    for copy in copies:
+        copy.wait_send()
+
+def reduce_all(g):
+    n = g.shape[-1]
+    vm = lambda *s: pltpu.VMEM(s + (n,), jnp.float32)
+    count = 3 + 9 * 6 + 3
+    return pl.pallas_call(reduce_kernel, out_shape=jax.ShapeDtypeStruct(g.shape, jnp.float32),
+        in_specs=[pl.BlockSpec(memory_space=pltpu.VMEM)], out_specs=pl.BlockSpec(memory_space=pltpu.VMEM),
+        scratch_shapes=[vm(2880), vm(3, 3, 240), vm(3, 256), vm(3, 3, 64), vm(3, 64), vm(3, 3, 16), vm(3, 256),
+                        pltpu.SemaphoreType.DMA((count,)), pltpu.SemaphoreType.DMA((count,))],
+        compiler_params=pltpu.CompilerParams(collective_id=0, has_side_effects=True, vmem_limit_bytes=50*1024*1024))(g)
+
+
+def group_sum_kernel(axis, n, in_ref, o_ref, arrived, send, recv):
+    me = lax.axis_index(axis)
+    rows = in_ref.shape[0] // n
+    others = [(me + k) % n for k in range(1, n)]
+    greet([{axis: to} for to in others])
+    copies = []
+    def start(src, dst, to):
+        i = len(copies)
+        copy = pltpu.make_async_remote_copy(src_ref=src, dst_ref=dst, send_sem=send.at[i], recv_sem=recv.at[i],
+            device_id={axis: to}, device_id_type=pl.DeviceIdType.MESH)
+        copy.start()
+        copies.append(copy)
+    for k, to in enumerate(others):
+        start(in_ref.at[pl.ds(pl.multiple_of(to * rows, 8), rows)], arrived.at[k], to)
+    for copy in copies:
+        copy.wait_recv()
+    mine = pl.multiple_of(me * rows, 8)
+    add_rows(o_ref, mine, [(in_ref, mine)] + [(arrived.at[k], 0) for k in range(n - 1)], rows, rows)
+    here = o_ref.at[pl.ds(mine, rows)]
+    for to in others:
+        start(here, here, to)
+    for copy in copies[n - 1:]:
+        copy.wait_recv()
+    for copy in copies:
+        copy.wait_send()
+
+def group_sum(value, axis, n, collective_id):
+    rows, cols = value.shape
+    return pl.pallas_call(functools.partial(group_sum_kernel, axis, n),
+        out_shape=jax.ShapeDtypeStruct(value.shape, jnp.float32),
+        in_specs=[pl.BlockSpec(memory_space=pltpu.VMEM)], out_specs=pl.BlockSpec(memory_space=pltpu.VMEM),
+        scratch_shapes=[pltpu.VMEM((n - 1, rows // n, cols), jnp.float32),
+                        pltpu.SemaphoreType.DMA((2 * n - 2,)), pltpu.SemaphoreType.DMA((2 * n - 2,))],
+        compiler_params=pltpu.CompilerParams(collective_id=collective_id, has_side_effects=True))(value)
+
+ORDERS = ((0, 1, 2), (1, 2, 0), (2, 0, 1))
+
+def spread_kernel(in_ref, o_ref, send, recv):
+    core, place = coords()
+    sibling = device_at(1 - core, place)
+    partners = [sibling]
+    for axis in range(3):
+        for step in (1, 2, 3):
+            partners.append(device_at(core, shifted_place(place, axis, step)))
+    greet(partners)
+    copies = []
+    def start(here, to):
+        i = len(copies)
+        copy = pltpu.make_async_remote_copy(src_ref=here, dst_ref=here, send_sem=send.at[i], recv_sem=recv.at[i],
+            device_id=to, device_id_type=pl.DeviceIdType.MESH)
+        copy.start()
+        copies.append(copy)
+        return copy
+    pending = [[] for _ in range(3)]
+    for level in (2, 1, 0):
+        for p in range(3):
+            for copy in pending[p]:
+                copy.wait_recv()
+            row, size = 0, 1024
+            for axis in ORDERS[p][:level + 1]:
+                size = size // 4
+                row = row + place[axis] * size
+            row = pl.multiple_of(row, 16)
+            if level == 2:
+                o_ref[core, p, pl.ds(row, 16), :] = in_ref[pl.ds(16 * p, 16), :]
+            here = o_ref.at[core, p, pl.ds(row, size)]
+            pending[p] = [start(here, device_at(core, shifted_place(place, ORDERS[p][level], s))) for s in (1, 2, 3)]
+    last = []
+    for p in range(3):
+        for copy in pending[p]:
+            copy.wait_recv()
+        last.append(start(o_ref.at[core, p], sibling))
+    for copy in last:
+        copy.wait_recv()
+    for copy in copies:
+        copy.wait_send()
+
+def spread(rows, collective_id):
+    return pl.pallas_call(spread_kernel, out_shape=jax.ShapeDtypeStruct((2, 3, 1024, rows.shape[1]), jnp.float32),
+        in_specs=[pl.BlockSpec(memory_space=pltpu.VMEM)], out_specs=pl.BlockSpec(memory_space=pltpu.VMEM),
+        scratch_shapes=[pltpu.SemaphoreType.DMA((30,)), pltpu.SemaphoreType.DMA((30,))],
+        compiler_params=pltpu.CompilerParams(collective_id=collective_id, has_side_effects=True, vmem_limit_bytes=40*1024*1024))(rows)
+
+def assemble(spread_out, full_rows):
+    n = spread_out.shape[-1]
+    parts = []
+    for p in range(3):
+        block = spread_out[:, p]
+        shape, names = [], []
+        for axis in ORDERS[p]:
+            shape += [2, 2] if axis == 1 else [4]
+            names += ["yh", "yl"] if axis == 1 else [["x", None, "z"][axis]]
+        block = block.reshape([2] + shape + [16, n])
+        perm = [1 + names.index(w) for w in ("z", "yh", "x", "yl")]
+        parts.append(block.transpose([0] + perm + [5, 6]))
+    both = jnp.stack(parts, axis=5)
+    both = both.reshape(2, 8, 384, n)[:, :, :full_rows // 8]
+    return both.reshape(2, full_rows, n)
+
+
 def with_rims(stacked):
     return padded_2(stacked, (("space", 3),), 1)
 
 
 def local(inputs, preacts, cotangent, weights, left_stats, left_basis, right_stats, right_basis):
-    layer_total = left_stats.shape[0]
     row_share = left_stats.shape[1]
     col_share = left_stats.shape[2]
     channels = inputs.shape[-1]
     full_rows = weights.shape[1]
     dp_index = lax.axis_index("dp")
     space_index = lax.axis_index("space")
-    layer_inputs = [inputs] + [jax.nn.silu(preacts[0].astype(jnp.float32)).astype(jnp.bfloat16)]
-    left_outs = [None] * layer_total
-    basis_outs = [None] * layer_total
-    right_outs = [None] * layer_total
-    turned_outs = [None] * layer_total
-
-    pieces = [None] * layer_total
-    current = cotangent
-    for layer_num in range(layer_total - 1, -1, -1):
-        if layer_num > 0:
-            extended = with_rims(jnp.stack([layer_inputs[layer_num], current]))
-            backward = input_grad(extended[1], weights[layer_num - 1])
-            following = (backward * silu_slope(preacts[layer_num - 1])).astype(jnp.bfloat16)
-        else:
-            extended = with_rims(layer_inputs[0][None])
-            following = current
-        gradient = weight_grad(extended[0], current)
-        complete = lax.psum(gradient, ("dp", "space"))
-        row_block = lax.dynamic_slice_in_dim(complete, space_index * row_share, row_share, 0)
-        col_block = lax.dynamic_slice_in_dim(complete, dp_index * col_share, col_share, 0)
-        gram_right = lax.dot_general(row_block, row_block, CONTRACT_ROWS, precision=HIGHEST)
-        left_new = BETA * left_stats[layer_num] + (1.0 - BETA) * lax.dot_general(
-            row_block, col_block, CONTRACT_COLS, precision=HIGHEST
-        )
-        left_outs[layer_num] = left_new
-        product_rows = lax.psum(jnp.dot(left_new, left_basis[layer_num], precision=HIGHEST), "dp")
-        gram_left = lax.dot_general(product_rows, product_rows, CONTRACT_ROWS, precision=HIGHEST)
-        summed_left, summed_right = lax.psum((gram_left, gram_right), "space")
-        right_new = BETA * right_stats[layer_num] + (1.0 - BETA) * summed_right
-        right_rows = jnp.dot(right_new, right_basis[layer_num], precision=HIGHEST)
-        right_gram = lax.dot_general(right_rows, right_rows, CONTRACT_ROWS, precision=HIGHEST)
-        right_outs[layer_num] = right_new
-        pieces[layer_num] = (product_rows, summed_left, right_rows, right_gram)
-        current = following
-    inverses = chol_inv(
-        jnp.stack([p[1] for p in pieces] + [p[3] for p in pieces])
-    )
-    for i in range(layer_total):
-        rows = math.sqrt(full_rows) * lax.dot_general(
-            pieces[i][0], inverses[i], CONTRACT_COLS, precision=HIGHEST
-        )
-        basis_outs[i] = lax.all_gather(rows, "space", axis=0, tiled=True)
-        turned_outs[i] = math.sqrt(channels) * lax.dot_general(
-            pieces[i][2], inverses[layer_total + i], CONTRACT_COLS, precision=HIGHEST
-        )
-    return (
-        jnp.stack(left_outs),
-        jnp.stack(basis_outs),
-        jnp.stack(right_outs),
-        jnp.stack(turned_outs),
-    )
+    stat_rows = lax.psum(
+        lax.dot_general(left_stats, left_basis, (((2,), (1,)), ((0,), (0,))), precision=HIGHEST), "dp"
+    )
+    full_basis = lax.all_gather(left_basis, "dp", axis=1, tiled=True)
+
+    activation = jax.nn.silu(preacts[0].astype(jnp.float32)).astype(jnp.bfloat16)
+    extended = with_rims(jnp.stack([activation, cotangent]))
+    backward = input_grad(extended[1], weights[0])
+    following = (backward * silu_slope(preacts[0])).astype(jnp.bfloat16)
+    first = with_rims(inputs[None])
+    gradient = jnp.stack([weight_grad(first[0], following), weight_grad(extended[0], cotangent)])
+    complete = reduce_all(gradient)
+
+    row_block = lax.dynamic_slice_in_dim(complete, space_index * row_share, row_share, 1)
+    col_block = lax.dynamic_slice_in_dim(complete, dp_index * col_share, col_share, 1)
+    left_new = BETA * left_stats + (1.0 - BETA) * lax.dot_general(
+        row_block, col_block, (((2,), (2,)), ((0,), (0,))), precision=HIGHEST
+    )
+    inner = (((1,), (1,)), ((0,), (0,)))
+    gram_right = lax.dot_general(complete, complete, inner, precision=HIGHEST)
+    turned = lax.dot_general(complete, full_basis, inner, precision=HIGHEST)
+    product_rows = BETA * stat_rows + (1.0 - BETA) * jnp.matmul(row_block, turned, precision=HIGHEST)
+    gram_left = lax.dot_general(product_rows, product_rows, inner, precision=HIGHEST)
+    gram_left = group_sum(gram_left.reshape(2 * channels, channels), "space", 8, 1)
+    right_new = BETA * right_stats + (1.0 - BETA) * gram_right
+    right_rows = jnp.matmul(right_new, right_basis, precision=HIGHEST)
+    right_gram = lax.dot_general(right_rows, right_rows, inner, precision=HIGHEST)
+    inverses = chol_inv(jnp.concatenate([gram_left.reshape(2, channels, channels), right_gram]))
+
+    core = dp_index % 2
+    place = ((dp_index // 2) % 4) * 2 + dp_index // 8
+    padded = jnp.pad(product_rows, ((0, 0), (0, 384 - row_share), (0, 0)))
+    own = lax.dynamic_slice(padded, (core, place * 48, 0), (1, 48, channels))[0]
+    own_inverse = lax.dynamic_index_in_dim(inverses[:2], core, 0, keepdims=False)
+    basis_rows = math.sqrt(full_rows) * lax.dot_general(
+        own, own_inverse, CONTRACT_COLS, precision=HIGHEST
+    )
+    basis_out = assemble(spread(basis_rows, 2), full_rows)
+    turned_out = math.sqrt(channels) * jnp.matmul(
+        right_rows, jnp.swapaxes(inverses[2:], 1, 2), precision=HIGHEST
+    )
+    return left_new, basis_out, right_new, turned_out
 
 
 def solution(mesh):

time: 782 us -> 462 us (0.59)
  waiting for transfers between devices: 502 us -> 4.93 us
  Pallas kernels: 36.5 us -> 207 us
  matrix products: 71.5 us -> 94.7 us
  local copies, waits for them, and re-layouts: 117 us -> 105 us
    psum x3 -> x1, waiting for transfers between devices: 378 us -> 0.02 us  [local(): lax.psum(lax.dot_general(left_stats, left_basis, (((2,), (1,)), ((0,), (0...]
    pallas_call x0 -> x3, Pallas kernels: none -> 170 us  [the longest x1 96 us: reduce_all(): pl.pallas_call(reduce_kernel, out_shape=jax.ShapeDtypeStruct(g.shape, jnp...]
    all_gather x2 -> x1, waiting for transfers between devices: 118 us -> 0.01 us  [local(): full_basis = lax.all_gather(left_basis, 'dp', axis=1, tiled=True)]
    dot_general x16 -> x10, matrix products: 31.5 us -> 66.6 us  [the longest x1 23.5 us: local(): gram_right = lax.dot_general(complete, complete, inner, precision=HIGHEST)]
    dot_general x18, matrix products: 30.1 us -> 17.2 us  [weight_grad(): lax.dot_general(shifted.reshape(-1, channels), flat_grad, CONTRACT_ROWS,...]
    all_gather x2 -> x0, local copies, waits for them, and re-layouts: 12.6 us -> none  [local(): basis_outs[i] = lax.all_gather(rows, 'space', axis=0, tiled=True)]
    concatenate x2 -> x0, local copies, waits for them, and re-layouts: 9.22 us -> none  [weight_grad(): return jnp.concatenate(blocks, axis=0)]
    unnamed x75 -> x48, local copies, waits for them, and re-layouts: 7.42 us -> 15.7 us
  transfers between devices with their start and end apart: 9 -> 6, of which waited for: 7 -> 1; matrix products, arithmetic and copies ran while one was open for 5% -> 38% of each run, Pallas kernels for 0% -> 21%
where the time goes in v2:
time: 462 us; the launch traced here: 458 us
  Pallas kernels  207 us (45%)
  local copies, waits for them, and re-layouts  105 us (23%)
  matrix products  94.7 us (20%)
  starting transfers between devices  16 us (3%)
  other arithmetic  14.9 us (3%)
  between operations  14.8 us (3%)
  waiting for transfers between devices  4.93 us (1%)
    pallas_call x1, Pallas kernels, reduce_all(): pl.pallas_call(reduce_kernel, out_shape=jax.ShapeDtypeStruct(g.shape, jnp...  96 us
    pallas_call x1, Pallas kernels, spread(): pl.pallas_call(spread_kernel, out_shape=jax.ShapeDtypeStruct((2, 3, 1024,...  42 us
    pallas_call x1, Pallas kernels, chol_inv(): pl.pallas_call(chol_inv_kernel, out_shape=jax.ShapeDtypeStruct(grams.shap...  36.7 us
    pallas_call x1, Pallas kernels, group_sum(): pl.pallas_call(functools.partial(group_sum_kernel, axis, n), out_shape=ja...  32.2 us
    reshape x9, local copies, waits for them, and re-layouts, input_grad(): shifted.reshape(-1, channels)  32 us
    slice x10, local copies, waits for them, and re-layouts, input_grad(): padded[:, :, 1 - row_step:1 - row_step + row_count, 1 - col_step:1 - col_...  31.1 us
    dot_general x1, matrix products, local(): gram_right = lax.dot_general(complete, complete, inner, precision=HIGHEST)  23.5 us
    dot_general x1, matrix products, local(): turned = lax.dot_general(complete, full_basis, inner, precision=HIGHEST)  21.8 us
  transfers between devices with their start and end apart: 6, of which 1 were waited for; matrix products, arithmetic and copies ran while one was open for 38% of the time, Pallas kernels for 21%

profile of v2, /device:TPU:1, one launch (start us, length us, event | category | flops | bytes accessed | tf_op | source)
XLA Modules:
  0.0 457.6 jit_solution(10293924289509780578)
XLA Ops:
  8.0 2.2 multiply_convert_fusion
  12.3 6.3 %collective-permute-start.2 = (bf16[2,1,1,1,240,320]{4,5,3,2,1,0:T(8,128)(2,1)S(1)}, bf16[2,1,1,1,240,320]{4,5,3,2,1,0:T(8,128)(2,1)S(1)}, u32[]{:S(2)}, u32[]{:S(2)}) collective-permute-start(bf16[2,1,1,1,240,320]{4,5,3,2,1,0:T(8,128)(2,1)S(1)} %get-tuple-element.21), channel_id=1, source_target_pairs={{0,1},{1,2},{2,3},{3,4},{4,5},{5,6},{6,7},{8,9},{9,10},{10,11},{11... | collective-permute-start | bytes 921608 | tf_op jit(solution)/shard_map/ppermute | solution.py:25
  21.6 7.0 %collective-permute-start = (bf16[1,1,1,1,240,320]{4,5,3,2,1,0:T(8,128)(2,1)}, bf16[1,1,1,1,240,320]{4,5,3,2,1,0:T(8,128)(2,1)}, u32[]{:S(2)}, u32[]{:S(2)}) collective-permute-start(bf16[1,1,1,1,240,320]{4,5,3,2,1,0:T(8,128)(2,1)} %get-tuple-element.32), channel_id=1, source_target_pairs={{0,1},{1,2},{2,3},{3,4},{4,5},{5,6},{6,7},{8,9},{9,10},{10,11},{11... | collective-permute-start | bytes 460808 | tf_op jit(solution)/shard_map/ppermute | solution.py:25
  28.7 2.4 fusion.193
  31.1 3.6 copy.111
  34.7 4.3 reshape.238
  38.9 4.2 collective-permute-done.1
  43.1 2.9 maximum_bitcast_fusion
  55.2 2.1 copy-done.11
  57.3 5.5 %pad_slice_fusion = (bf16[1,1,8,240,320]{3,4,2,1,0:T(8,128)(2,1)S(1)}, bf16[1,1,8,240,320]{3,4,2,1,0:T(8,128)(2,1)}, bf16[1,1,8,240,320]{3,4,2,1,0:T(8,128)(2,1)...) fusion(bf16[1,1,10,240,320]{3,4,2,1,0:T(8,128)(2,1)S(1)} %get-t, ...), kind=kLoop, calls=%fused_computation.134 | loop fusion | bytes 16629760 | tf_op jit(solution)/shard_map/slice | solution.py:76
  64.7 3.4 reshape.207
  68.1 3.2 copy.103
  71.2 3.7 reshape.208
  74.9 3.1 copy.104
  78.1 3.6 reshape.209
  81.7 3.1 copy.105
  84.8 3.7 reshape.210
  88.5 3.1 copy.106
  91.6 3.7 reshape.211
  95.2 3.1 copy.107
  98.4 3.7 reshape.212
  102.1 3.1 copy.108
  105.2 3.6 reshape.213
  108.8 3.2 copy.109
  112.0 3.8 reshape.214
  117.6 2.8 reshape.215
  131.9 2.5 fusion.3
  134.4 4.5 convert_element_type.61
  139.0 2.3 fusion.61
  148.4 4.0 pad_maximum_fusion.1.g_ref
  152.5 96.0 %shard_map.111 = f32[2,2880,320]{2,1,0:T(8,128)} custom-call(f32[2,2880,320]{2,1,0:T(8,128)} %pad_maximum_fusion.1.g_ref), custom_call_target="tpu_custom_call" | custom-call | tf_op jit(solution)/shard_map/pallas_call | solution.py:285
  248.5 23.5 %fusion.56 = f32[2,320,320]{2,1,0:T(8,128)S(1)} fusion(f32[2,2880,320]{2,1,0:T(8,128)} %shard_map.111, f32[2,320,320]{2,1,0:T(8,128)S(1)} %copy-done.20), kind=kOutput, calls=%fused_computation.84 | convolution fusion | flops 7078502400 | bytes 9011200 | tf_op jit(solution)/shard_map/dot_general | solution.py:422
  272.0 2.0 fusion.248
  274.0 3.1 fusion.249
  277.1 2.9 fusion.57
  281.2 21.8 %fusion = f32[2,320,320]{1,2,0:T(8,128)} fusion(f32[2,2880,320]{2,1,0:T(8,128)} %shard_map.111, f32[2,2880,320]{2,0,1:T(2,128)} %all-gather.2.cloned.1.call-done), kind=kOutput, calls=%fused_computation.2 | convolution fusion | flops 7077888000 | bytes 15564800 | tf_op jit(solution)/shard_map/dot_general | solution.py:423
  303.0 4.0 fusion.4
  307.0 3.1 fusion.247
  310.1 32.2 %shard_map.112 = f32[640,320]{1,0:T(8,128)} custom-call(f32[640,320]{1,0:T(8,128)} %bitcast.394), custom_call_target="tpu_custom_call" | custom-call | tf_op jit(solution)/shard_map/pallas_call | solution.py:320
  343.9 36.7 %shard_map.113 = f32[4,320,320]{2,1,0:T(8,128)S(1)} custom-call(f32[4,320,320]{2,1,0:T(8,128)S(1)} %pad_maximum_fusion.3.g_ref), custom_call_target="tpu_custom_call" | custom-call | tf_op jit(solution)/shard_map/pallas_call | solution.py:156
  380.7 3.1 convolution_multiply_fusion
  384.6 42.0 %shard_map.114 = f32[2,3,1024,320]{3,2,1,0:T(8,128)S(1)} custom-call(f32[48,320]{1,0:T(8,128)S(1)} %convolution_multiply_fusion.4.in_ref), custom_call_target="tpu_custom_call" | custom-call | tf_op jit(solution)/shard_map/pallas_call | solution.py:370
  426.6 3.3 fusion.245
  429.9 2.3 copy.225
  433.1 2.1 copy.227
  435.3 2.4 pad_maximum_fusion
  437.7 4.1 slice.251
  441.8 8.8 %copy.153 = f32[2,2880,320]{1,2,0:T(8,128)} copy(f32[2,2880,320]{2,1,0:T(8,128)} %bitcast.381) | data formatting | bytes 14745600
  (93 shorter events, 41.6 us)
Async XLA Ops:
  7.2 264.8 %copy-start = (f32[2,320,320]{2,1,0:T(8,128)S(1)}, f32[2,320,320]{2,1,0:T(8,128)}, u32[]{:S(2)}) copy-start(f32[2,320,320]{2,1,0:T(8,128)} %param.15) | copy-start | bytes 2457604
  7.2 274.0 %all-gather.2.cloned.1.call-start = ((), (), s32[]{:S(2)}) async-start(), calls=%async_computation.1 | async-start | bytes 9400320 | tf_op jit(solution)/shard_map/all_gather | solution.py:406
  7.9 295.1 %all-reduce.6.cloned.1.call-start = ((), (), s32[]{:S(2)}) async-start(), calls=%async_computation | async-start | bytes 1966080 | tf_op jit(solution)/shard_map/psum | solution.py:403
  8.0 2.2 copy-start.2
  10.1 18.5 %copy-start.14 = (f32[2,360,180]{1,0,2:T(2,128)S(1)}, f32[2,360,180]{1,0,2:T(2,128)}, u32[]{:S(2)}) copy-start(f32[2,360,180]{1,0,2:T(2,128)} %param.12) | copy-start | bytes 1555204
  10.1 18.5 %copy-start.16 = (f32[2,180,320]{2,0,1:T(2,128)S(1)}, f32[2,180,320]{2,0,1:T(2,128)}, u32[]{:S(2)}) copy-start(f32[2,180,320]{2,0,1:T(2,128)} %param.13) | copy-start | bytes 1382404
  11.0 35.0 %collective-permute-start.3 = (bf16[2,1,1,1,240,320]{4,5,3,2,1,0:T(8,128)(2,1)}, bf16[2,1,1,1,240,320]{4,5,3,2,1,0:T(8,128)(2,1)S(1)}, u32[]{:S(2)}, u32[]{:S(2)}) collective-permute-start(bf16[2,1,1,1,240,320]{4,5,3,2,1,0:T(8,128)(2,1)} %get-tuple-element.22), channel_id=1, source_target_pairs={{1,0},{2,1},{3,2},{4,3},{5,4},{6,5},{7,6},{9,8},{10,9},{11,10},{12... | collective-permute-start | bytes 921608 | tf_op jit(solution)/shard_map/ppermute | solution.py:26
  12.3 33.7 %collective-permute-start.2 = (bf16[2,1,1,1,240,320]{4,5,3,2,1,0:T(8,128)(2,1)S(1)}, bf16[2,1,1,1,240,320]{4,5,3,2,1,0:T(8,128)(2,1)S(1)}, u32[]{:S(2)}, u32[]{:S(2)}) collective-permute-start(bf16[2,1,1,1,240,320]{4,5,3,2,1,0:T(8,128)(2,1)S(1)} %get-tuple-element.21), channel_id=1, source_target_pairs={{0,1},{1,2},{2,3},{3,4},{4,5},{5,6},{6,7},{8,9},{9,10},{10,11},{11... | collective-permute-start | bytes 921608 | tf_op jit(solution)/shard_map/ppermute | solution.py:25
  20.3 22.8 %collective-permute-start.1 = (bf16[1,1,1,1,240,320]{4,5,3,2,1,0:T(8,128)(2,1)}, bf16[1,1,1,1,240,320]{4,5,3,2,1,0:T(8,128)(2,1)S(1)}, u32[]{:S(2)}, u32[]{:S(2)}) collective-permute-start(bf16[1,1,1,1,240,320]{4,5,3,2,1,0:T(8,128)(2,1)} %get-tuple-element.33), channel_id=1, source_target_pairs={{1,0},{2,1},{3,2},{4,3},{5,4},{6,5},{7,6},{9,8},{10,9},{11,10},{12... | collective-permute-start | bytes 460808 | tf_op jit(solution)/shard_map/ppermute | solution.py:26
  21.6 21.5 %collective-permute-start = (bf16[1,1,1,1,240,320]{4,5,3,2,1,0:T(8,128)(2,1)}, bf16[1,1,1,1,240,320]{4,5,3,2,1,0:T(8,128)(2,1)}, u32[]{:S(2)}, u32[]{:S(2)}) collective-permute-start(bf16[1,1,1,1,240,320]{4,5,3,2,1,0:T(8,128)(2,1)} %get-tuple-element.32), channel_id=1, source_target_pairs={{0,1},{1,2},{2,3},{3,4},{4,5},{5,6},{6,7},{8,9},{9,10},{10,11},{11... | collective-permute-start | bytes 460808 | tf_op jit(solution)/shard_map/ppermute | solution.py:25
  38.9 7.1 %copy-start.3 = (bf16[1,1,8,240,320]{3,4,2,1,0:T(8,128)(2,1)S(1)}, bf16[1,1,8,240,320]{3,4,2,1,0:T(8,128)(2,1)}, u32[]{:S(2)}) copy-start(bf16[1,1,8,240,320]{3,4,2,1,0:T(8,128)(2,1)} %param.10) | copy-start | bytes 3686404
  55.2 2.1 copy-start.11
  120.4 2.0 copy-start.4
  120.4 2.0 copy-start.17
  122.4 1.3 copy-start.5
  123.7 1.3 copy-start.6
  125.0 1.3 copy-start.7
  126.3 1.3 copy-start.8
  127.6 1.3 copy-start.9
  128.9 1.3 copy-start.10
  130.2 1.7 copy-start.13
  134.4 4.5 copy-start.18
  139.0 2.3 copy-start.19
  145.7 2.7 slice-start
  146.6 1.8 slice-start.1
  152.5 96.0 %copy-start.20 = (f32[2,320,320]{2,1,0:T(8,128)S(1)}, f32[2,320,320]{2,1,0:T(8,128)}, u32[]{:S(2)}) copy-start(f32[2,320,320]{2,1,0:T(8,128)} %param.14) | copy-start | bytes 2457604
  272.0 5.1 %copy-start.12 = (f32[2,320,320]{2,1,0:T(8,128)}, f32[2,320,320]{2,1,0:T(8,128)S(1)}, u32[]{:S(2)}) copy-start(f32[2,320,320]{2,1,0:T(8,128)S(1)} %fusion.56) | copy-start | bytes 2457604
  274.0 3.1 copy-start.15
  429.9 2.8 copy-start.1
Sparse Core Ops, SparseCore 0:
  9.7 65.2 all-gather.1
  77.5 130.7 all-reduce.5

commit v3 on v1

v3 whole, which is shorter than its diff:
```python
import functools
import math

import jax
import jax.numpy as jnp
from jax import lax
from jax.experimental import pallas as pl
from jax.experimental.pallas import tpu as pltpu
from jax.sharding import PartitionSpec as P

BETA = 0.95
HIGHEST = lax.Precision.HIGHEST
CONTRACT_ROWS = (((0,), (0,)), ((), ()))
CONTRACT_COLS = (((1,), (1,)), ((), ()))
MESH = pl.DeviceIdType.MESH
ORDERS = ((0, 1, 2), (1, 2, 0), (2, 0, 1))
PADDED = 384


def kernel_params(collective_id=None):
    extra = {} if collective_id is None else {"collective_id": collective_id, "has_side_effects": True}
    return pltpu.CompilerParams(vmem_limit_bytes=50 * 1024 * 1024, **extra)

def coords():
    dp, space = lax.axis_index("dp"), lax.axis_index("space")
    core, x, y = dp % 2, (dp // 2) % 4, (space % 2) * 2 + dp // 8
    return core, (x, y, space // 2)

def device_at(core, place):
    x, y, z = place
    return {"dp": ((y % 2) * 4 + x) * 2 + core, "space": z * 2 + y // 2}

def shifted_place(place, axis, step):
    moved = list(place)
    moved[axis] = (place[axis] + step) % 4
    return tuple(moved)

def greet(partners):
    barrier = pltpu.get_barrier_semaphore()
    for partner in partners:
        pl.semaphore_signal(barrier, inc=1, device_id=partner, device_id_type=pl.DeviceIdType.MESH)
    pl.semaphore_wait(barrier, len(partners))

def add_rows(dst, dst_row, terms, rows, step):
    def body(i, carry):
        total = None
        for ref, start in terms:
            first = pl.multiple_of(start + i * step, 8)
            value = ref[pl.ds(first, step), :]
            total = value if total is None else total + value
        dst[pl.ds(pl.multiple_of(dst_row + i * step, 8), step), :] = total
        return carry
    lax.fori_loop(0, rows // step, body, 0)


class Sender:
    def __init__(self, send, recv):
        self.send, self.recv, self.copies = send, recv, []

    def start(self, src, dst, to):
        n = len(self.copies)
        copy = pltpu.make_async_remote_copy(
            src_ref=src, dst_ref=dst, send_sem=self.send.at[n], recv_sem=self.recv.at[n],
            device_id=to, device_id_type=MESH,
        )
        copy.start()
        self.copies.append(copy)
        return copy

    def finish(self):
        for copy in self.copies:
            copy.wait_send()


def arrived(copies):
    for copy in copies:
        copy.wait_recv()


def all_partners(core, place):
    partners = [device_at(1 - core, place)]
    for axis in range(3):
        for step in (1, 2, 3):
            partners.append(device_at(core, shifted_place(place, axis, step)))
    return partners


def moved_to(place, axis, value):
    moved = list(place)
    moved[axis] = value
    return tuple(moved)


def ring_pairs(half):
    near = lambda x: x + 1 - 2 * (x % 2)
    far = lambda x: 3 - x
    return (near, far) if half == 0 else (far, near)


def peers(place, axis):
    return [shifted_place(place, axis, step) for step in (1, 2, 3)]


def reduce_kernel(g_ref, o_ref, r0, r1, s1, b, r2, c, r3, f, send, recv):
    core, place = coords()
    greet(all_partners(core, place))
    sibling = device_at(1 - core, place)
    out = Sender(send, recv)
    part, chunk, half_rows = 960, 240, 120
    first = [out.start(g_ref.at[1 - core, pl.ds(p * part, part)], r0.at[pl.ds(p * part, part)], sibling) for p in range(3)]
    level1a, level1b, level2, level3 = {}, {}, [], []

    def rows_at(p, j, half):
        return pl.multiple_of(p * part + j * chunk + half * half_rows, 8)

    for p in range(3):
        first[p].wait_recv()
        add_rows(r0, p * part, [(r0, p * part), (g_ref.at[core], p * part)], part, 96)
        axis = ORDERS[p][0]
        for half in range(2):
            near, far = ring_pairs(half)
            to = near(place[axis])
            device = device_at(core, moved_to(place, axis, to))
            level1a[p, half] = [
                out.start(r0.at[pl.ds(rows_at(p, j, half), half_rows)], r1.at[p, half, slot], device)
                for slot, j in ((1, far(to)), (0, to))
            ]
    for p in range(3):
        axis = ORDERS[p][0]
        for half in range(2):
            near, far = ring_pairs(half)
            to = far(place[axis])
            level1a[p, half][0].wait_recv()
            add_rows(s1.at[p, half], 0, [(r0, rows_at(p, to, half)), (r1.at[p, half, 1], 0)], half_rows, 40)
            level1b[p, half] = out.start(s1.at[p, half], r1.at[p, half, 2], device_at(core, moved_to(place, axis, to)))
    for p in range(3):
        mine = place[ORDERS[p][0]]
        for half in range(2):
            level1a[p, half][1].wait_recv()
            level1b[p, half].wait_recv()
            add_rows(b.at[p], half * half_rows,
                     [(r0, rows_at(p, mine, half)), (r1.at[p, half, 0], 0), (r1.at[p, half, 2], 0)], half_rows, 40)
        b[p, chunk:, :] = jnp.zeros((16, b.shape[2]), jnp.float32)
        axis = ORDERS[p][1]
        level2.append([
            out.start(b.at[p, pl.ds(pl.multiple_of(to[axis] * 64, 8), 64)], r2.at[p, k], device_at(core, to))
            for k, to in enumerate(peers(place, axis))
        ])
    for p in range(3):
        arrived(level2[p])
        mine = place[ORDERS[p][1]]
        add_rows(c.at[p], 0, [(b.at[p], mine * 64)] + [(r2.at[p, k], 0) for k in range(3)], 64, 64)
        axis = ORDERS[p][2]
        level3.append([
            out.start(c.at[p, pl.ds(pl.multiple_of(to[axis] * 16, 8), 16)], r3.at[p, k], device_at(core, to))
            for k, to in enumerate(peers(place, axis))
        ])
    gather3, gather2, gather1a, gather1b, last = [], [], {}, {}, []
    for p in range(3):
        arrived(level3[p])
        axis = ORDERS[p][2]
        row = pl.multiple_of(place[ORDERS[p][1]] * 64 + place[axis] * 16, 8)
        add_rows(f.at[p], row, [(c.at[p], place[axis] * 16)] + [(r3.at[p, k], 0) for k in range(3)], 16, 16)
        here = f.at[p, pl.ds(row, 16)]
        gather3.append([out.start(here, here, device_at(core, to)) for to in peers(place, axis)])
    for p in range(3):
        arrived(gather3[p])
        axis = ORDERS[p][1]
        here = f.at[p, pl.ds(pl.multiple_of(place[axis] * 64, 8), 64)]
        gather2.append([out.start(here, here, device_at(core, to)) for to in peers(place, axis)])

    def gathered(p, j, half):
        return o_ref.at[core, pl.ds(rows_at(p, j, half), half_rows)]

    for p in range(3):
        arrived(gather2[p])
        axis = ORDERS[p][0]
        x = place[axis]
        add_rows(o_ref.at[core], rows_at(p, x, 0), [(f.at[p], 0)], chunk, 48)
        for half in range(2):
            near, far = ring_pairs(half)
            here = gathered(p, x, half)
            gather1a[p, half] = out.start(here, here, device_at(core, moved_to(place, axis, far(x))))
            gather1b[p, half] = [out.start(here, here, device_at(core, moved_to(place, axis, near(x))))]
    for p in range(3):
        axis = ORDERS[p][0]
        x = place[axis]
        for half in range(2):
            near, far = ring_pairs(half)
            gather1a[p, half].wait_recv()
            here = gathered(p, far(x), half)
            gather1b[p, half].append(out.start(here, here, device_at(core, moved_to(place, axis, near(x)))))
    for p in range(3):
        for half in range(2):
            arrived(gather1b[p, half])
        here = o_ref.at[core, pl.ds(p * part, part)]
        last.append(out.start(here, here, sibling))
    arrived(last)
    out.finish()


def reduce_all(g):
    n = g.shape[-1]
    vm = lambda *s: pltpu.VMEM(s + (n,), jnp.float32)
    count = 3 + 18 + 9 * 4 + 18 + 3
    return pl.pallas_call(
        reduce_kernel,
        out_shape=jax.ShapeDtypeStruct(g.shape, jnp.float32),
        in_specs=[pl.BlockSpec(memory_space=pltpu.VMEM)],
        out_specs=pl.BlockSpec(memory_space=pltpu.VMEM),
        scratch_shapes=[vm(2880), vm(3, 2, 3, 120), vm(3, 2, 120), vm(3, 256), vm(3, 3, 64), vm(3, 64), vm(3, 3, 16),
                        vm(3, 256), pltpu.SemaphoreType.DMA((count,)), pltpu.SemaphoreType.DMA((count,))],
        compiler_params=kernel_params(0),
    )(g)


def gram_kernel(p_ref, own_ref, gram_ref, r0, r1, a, b, r2, c, r3, f, r4, send, recv):
    core, place = coords()
    x, y, z = place
    quads = []
    for step in range(1, 8):
        quads.append(((x + step // 2) % 4, (y // 2) * 2 + (y + step % 2) % 2, z))
    partners = all_partners(core, place)
    partners += [device_at(core, to) for step, to in enumerate(quads, 1) if step // 2 and step % 2]
    greet(partners)
    out = Sender(send, recv)
    out.start(p_ref.at[1 - core], r0, device_at(1 - core, place)).wait_recv()
    add_rows(a, 0, [(r0, 0), (p_ref.at[core], 0)], PADDED, 96)
    block = lambda to: pl.multiple_of((to[0] * 2 + to[1] % 2) * 48, 16)
    arrived([out.start(a.at[pl.ds(block(to), 48)], r1.at[k], device_at(core, to)) for k, to in enumerate(quads)])
    add_rows(own_ref, 0, [(a, block(place))] + [(r1.at[k], 0) for k in range(7)], 48, 48)
    own = own_ref[...]
    n = own.shape[1]
    gram = lax.dot_general(own, own, CONTRACT_ROWS, precision=HIGHEST, preferred_element_type=jnp.float32)
    b[0, :, :] = gram[:128]
    b[1, :, :] = gram[128:256]
    b[2, :n - 256, :] = gram[256:]
    b[2, n - 256:, :] = jnp.zeros((PADDED - n, n), jnp.float32)
    level1, level2, level3, gather2, gather1 = [], [], [], [], []
    for p in range(3):
        axis = ORDERS[p][0]
        level1.append([
            out.start(b.at[p, pl.ds(pl.multiple_of(to[axis] * 32, 8), 32)], r2.at[p, k], device_at(core, to))
            for k, to in enumerate(peers(place, axis))
        ])
    for p in range(3):
        arrived(level1[p])
        add_rows(c.at[p], 0, [(b.at[p], place[ORDERS[p][0]] * 32)] + [(r2.at[p, k], 0) for k in range(3)], 32, 32)
        axis = ORDERS[p][1]
        level2.append([
            out.start(c.at[p, pl.ds(pl.multiple_of(to[axis] * 8, 8), 8)], r3.at[p, k], device_at(core, to))
            for k, to in enumerate(peers(place, axis))
        ])
    for p in range(3):
        arrived(level2[p])
        add_rows(f.at[p], 0, [(c.at[p], place[ORDERS[p][1]] * 8)] + [(r3.at[p, k], 0) for k in range(3)], 8, 8)
        axis = ORDERS[p][2]
        level3.append([
            out.start(f.at[p], r4.at[p, k], device_at(core, to)) for k, to in enumerate(peers(place, axis))
        ])
    for p in range(3):
        arrived(level3[p])
        axis = ORDERS[p][1]
        row = pl.multiple_of(p * 128 + place[ORDERS[p][0]] * 32 + place[axis] * 8, 8)
        add_rows(gram_ref, row, [(f.at[p], 0)] + [(r4.at[p, k], 0) for k in range(3)], 8, 8)
        here = gram_ref.at[pl.ds(row, 8)]
        gather2.append([out.start(here, here, device_at(core, to)) for to in peers(place, axis)])
    for p in range(3):
        arrived(gather2[p])
        axis = ORDERS[p][0]
        here = gram_ref.at[pl.ds(pl.multiple_of(p * 128 + place[axis] * 32, 8), 32)]
        gather1.append([out.start(here, here, device_at(core, to)) for to in peers(place, axis)])
    for p in range(3):
        arrived(gather1[p])
    out.finish()


def gram_of_rows(partial):
    n = partial.shape[-1]
    vm = lambda *s: pltpu.VMEM(s + (n,), jnp.float32)
    return pl.pallas_call(
        gram_kernel,
        out_shape=(jax.ShapeDtypeStruct((48, n), jnp.float32), jax.ShapeDtypeStruct((PADDED, n), jnp.float32)),
        in_specs=[pl.BlockSpec(memory_space=pltpu.VMEM)],
        out_specs=(pl.BlockSpec(memory_space=pltpu.VMEM),) * 2,
        scratch_shapes=[vm(PADDED), vm(7, 48), vm(PADDED), vm(3, 128), vm(3, 3, 32), vm(3, 32), vm(3, 3, 8), vm(3, 8),
                        vm(3, 3, 8), pltpu.SemaphoreType.DMA((53,)), pltpu.SemaphoreType.DMA((53,))],
        compiler_params=kernel_params(1),
    )(partial)


def spread_kernel(in_ref, x_ref, o_ref, y_ref, send, recv):
    core, place = coords()
    greet(all_partners(core, place))
    sibling = device_at(1 - core, place)
    out = Sender(send, recv)
    last = [out.start(x_ref, y_ref.at[core], sibling)]
    y_ref[core] = x_ref[...]

    def view(p, places, half=None):
        row, size = 0, 1024
        for c in places:
            size = size // 4
            row = row + c * size
        if half is not None:
            size = size // 2
            row = row + half * size
        return o_ref.at[core, p, pl.ds(pl.multiple_of(row, 16), size)]

    pending, gather1a, gather1b = [], {}, {}
    for p in range(3):
        a1, a2, a3 = ORDERS[p]
        here = view(p, (place[a1], place[a2], place[a3]))
        here[...] = in_ref[pl.ds(16 * p, 16), :]
        pending.append([out.start(here, here, device_at(core, to)) for to in peers(place, a3)])
    for p in range(3):
        arrived(pending[p])
        a1, a2, a3 = ORDERS[p]
        here = view(p, (place[a1], place[a2]))
        pending[p] = [out.start(here, here, device_at(core, to)) for to in peers(place, a2)]
    for p in range(3):
        arrived(pending[p])
        axis = ORDERS[p][0]
        x = place[axis]
        for half in range(2):
            near, far = ring_pairs(half)
            here = view(p, (x,), half)
            gather1a[p, half] = out.start(here, here, device_at(core, moved_to(place, axis, far(x))))
            gather1b[p, half] = [out.start(here, here, device_at(core, moved_to(place, axis, near(x))))]
    for p in range(3):
        axis = ORDERS[p][0]
        x = place[axis]
        for half in range(2):
            near, far = ring_pairs(half)
            gather1a[p, half].wait_recv()
            here = view(p, (far(x),), half)
            gather1b[p, half].append(out.start(here, here, device_at(core, moved_to(place, axis, near(x)))))
    for p in range(3):
        for half in range(2):
            arrived(gather1b[p, half])
        last.append(out.start(o_ref.at[core, p], o_ref.at[core, p], sibling))
    arrived(last)
    out.finish()


def spread(rows, extra):
    n = rows.shape[1]
    return pl.pallas_call(
        spread_kernel,
        out_shape=(jax.ShapeDtypeStruct((2, 3, 1024, n), jnp.float32),
                   jax.ShapeDtypeStruct((2,) + extra.shape, jnp.float32)),
        in_specs=[pl.BlockSpec(memory_space=pltpu.VMEM)] * 2,
        out_specs=(pl.BlockSpec(memory_space=pltpu.VMEM),) * 2,
        scratch_shapes=[pltpu.SemaphoreType.DMA((40,)), pltpu.SemaphoreType.DMA((40,))],
        compiler_params=kernel_params(2),
    )(rows, extra)


def assemble_kernel(in_ref, o_ref):
    layer, block = pl.program_id(0), pl.program_id(1)
    z, y_high = block // 2, block % 2
    for q in range(8):
        place = (q // 2, y_high * 2 + q % 2, z)
        for p in range(3):
            row = 48 * q + 16 * p
            size = min(16, o_ref.shape[1] - row)
            if size <= 0:
                continue
            a1, a2, a3 = ORDERS[p]
            src = pl.multiple_of(((place[a1] * 4 + place[a2]) * 4 + place[a3]) * 16, 16)
            o_ref[0, row:row + size, :] = in_ref[layer, p, pl.ds(src, size), :]


def assemble(spread_out, full_rows):
    n = spread_out.shape[-1]
    share = full_rows // 8
    return pl.pallas_call(
        assemble_kernel,
        grid=(2, 8),
        out_shape=jax.ShapeDtypeStruct((2, full_rows, n), jnp.float32),
        in_specs=[pl.BlockSpec(memory_space=pltpu.VMEM)],
        out_specs=pl.BlockSpec((1, share, n), lambda i, j: (i, j, 0)),
        compiler_params=kernel_params(),
    )(spread_out)


def three_wide(x):
    cols = x.shape[0]
    col = lax.broadcasted_iota(jnp.int32, x.shape, 0)
    before = jnp.where(col == 0, 0.0, pltpu.roll(x, 1, 0))
    after = jnp.where(col == cols - 1, 0.0, pltpu.roll(x, cols - 1, 0))
    return jnp.concatenate([v.astype(jnp.bfloat16) for v in (before, x, after)], axis=1)

def grads_kernel(remote, rows, cols, a_ref, v_ref, g_ref, w_ref, o_ref, rims, wide, wide_g, back, g_t, w_t, send, recv):
    n = a_ref.shape[1]
    copies = []
    if remote:
        me = lax.axis_index("space")
        up, down = (me + 7) % 8, (me + 1) % 8
        greet([{"space": up}, {"space": down}])
        for i, ref in enumerate((g_ref, v_ref, a_ref)):
            for side, (first, to) in enumerate((((rows - 1) * cols, down), (0, up))):
                copy = pltpu.make_async_remote_copy(src_ref=ref.at[pl.ds(first, cols)], dst_ref=rims.at[i, side],
                    send_sem=send.at[2 * i + side], recv_sem=recv.at[2 * i + side],
                    device_id={"space": to}, device_id_type=pl.DeviceIdType.MESH)
                copy.start()
                copies.append(copy)
        has = (me > 0, me < 7)
    else:
        has = (True, True)
    same = lambda x: x
    silu = lambda x: (x * jax.nn.sigmoid(x)).astype(jnp.bfloat16).astype(jnp.float32)
    def widen_rows(ref, dst, change):
        def body(r, carry):
            x = change(ref[pl.ds(pl.multiple_of(r * cols, 16), cols), :].astype(jnp.float32))
            dst[pl.ds(pl.multiple_of((r + 1) * cols, 16), cols), :] = three_wide(x)
            return carry
        lax.fori_loop(0, rows, body, 0)
    def widen_rims(i, dst, change):
        for side in range(2):
            if remote:
                copies[2 * i + side].wait_recv()
            x = change(rims[i, side].astype(jnp.float32))
            x = jnp.where(has[side], x, 0.0)
            dst[pl.ds(side * (rows + 1) * cols, cols), :] = three_wide(x)
    cells = rows * cols
    def gradient(layer):
        def body(dr, carry):
            start = pl.multiple_of(dr * cols, 16)
            for lane in range(0, 3 * n, 256):
                size = min(256, 3 * n - lane)
                part = jnp.dot(g_t[...], wide[pl.ds(start, cells), pl.ds(lane, size)],
                               preferred_element_type=jnp.float32)
                o_ref[layer, pl.ds(pl.multiple_of(dr * 3 * n + lane, 8), size), :] = part.T
            return carry
        lax.fori_loop(0, 3, body, 0)
    for dr in range(3):
        for seg in range(3):
            tap = w_ref[pl.ds((3 * dr + 2 - seg) * n, n), :]
            w_t[dr, pl.ds(seg * n, n), :] = tap.T
    widen_rows(v_ref, wide, silu)
    widen_rows(g_ref, wide_g, same)
    g_t[...] = g_ref[...].T
    widen_rims(0, wide_g, same)
    widen_rims(1, wide, silu)
    gradient(1)
    half = cells // 2
    def back_body(i, carry):
        first = pl.multiple_of(i * half, 16)
        total = None
        for dr in range(3):
            x = wide_g[pl.ds(pl.multiple_of(first + (2 - dr) * cols, 16), half), :]
            y = jnp.dot(x, w_t[dr], preferred_element_type=jnp.float32)
            total = y if total is None else total + y
        v = v_ref[pl.ds(first, half), :].astype(jnp.float32)
        s = jax.nn.sigmoid(v)
        back[pl.ds(first, half), :] = (total * (s * (1.0 + v * (1.0 - s)))).astype(jnp.bfloat16)
        return carry
    lax.fori_loop(0, 2, back_body, 0)
    g_t[...] = back[...].T
    widen_rows(a_ref, wide, same)
    widen_rims(2, wide, same)
    gradient(0)
    for copy in copies:
        copy.wait_send()

def gradients(inputs, preacts, cotangent, weights, remote=True, collective_id=3):
    rows, cols, n = inputs.shape
    flat = [x.reshape(rows * cols, n) for x in (inputs, preacts, cotangent)]
    b16 = jnp.bfloat16
    return pl.pallas_call(functools.partial(grads_kernel, remote, rows, cols),
        out_shape=jax.ShapeDtypeStruct((2, 9 * n, n), jnp.float32),
        in_specs=[pl.BlockSpec(memory_space=pltpu.VMEM)] * 4, out_specs=pl.BlockSpec(memory_space=pltpu.VMEM),
        scratch_shapes=[pltpu.VMEM((3, 2, cols, n), b16), pltpu.VMEM(((rows + 2) * cols, 3 * n), b16),
                        pltpu.VMEM(((rows + 2) * cols, 3 * n), b16), pltpu.VMEM((rows * cols, n), b16),
                        pltpu.VMEM((n, rows * cols), b16), pltpu.VMEM((3, 3 * n, n), b16),
                        pltpu.SemaphoreType.DMA((6,)), pltpu.SemaphoreType.DMA((6,))],
        compiler_params=kernel_params(collective_id if remote else None))(*flat, weights)


NB = 64

def diag_inverse(blocks):
    n = NB
    row = lax.broadcasted_iota(jnp.int32, (n, 2 * n), 0)
    col = lax.broadcasted_iota(jnp.int32, (n, 2 * n), 1)
    eye = jnp.where(row + n == col, 1.0, 0.0).astype(jnp.float32)
    tiles = []
    for b in blocks:
        x = jnp.concatenate([b, jnp.zeros((n, n), jnp.float32)], axis=1) + eye
        tiles.append([x[8 * t:8 * t + 8] for t in range(n // 8)])
    sub = lax.broadcasted_iota(jnp.int32, (8, 2 * n), 0)
    scales = [[None] * (n // 8) for _ in blocks]
    for j in range(n):
        tj, sj = j // 8, j % 8
        for m in range(len(blocks)):
            x = tiles[m]
            pivot_row = x[tj][sj:sj + 1, :]
            cb = jnp.broadcast_to(x[tj][:, j:j + 1], (8, 2 * n))
            d = cb[sj:sj + 1, :]
            rs = lax.rsqrt(d)
            scales[m][tj] = jnp.where(sub == sj, rs, scales[m][tj] if sj else 0.0)
            scaled = pivot_row * (rs * rs)
            if sj < 7:
                x[tj] = x[tj] - jnp.where(sub > sj, cb, 0.0) * scaled
            for t in range(tj + 1, n // 8):
                x[t] = x[t] - jnp.broadcast_to(x[t][:, j:j + 1], (8, 2 * n)) * scaled
    out = []
    for m in range(len(blocks)):
        w = jnp.concatenate([tiles[m][t] * scales[m][t] for t in range(n // 8)], axis=0)
        out.append(w[:, n:])
    return out

def chol_inv_kernel(g_ref, o_ref):
    nm, size, _ = g_ref.shape
    o_ref[...] = g_ref[...]
    nblk = size // NB
    for k in range(nblk):
        o = k * NB
        linv = diag_inverse([o_ref[m, o:o + NB, o:o + NB] for m in range(nm)])
        for m in range(nm):
            parts = []
            prow = o_ref[m, o:o + NB, :]
            r = jnp.dot(linv[m], prow, precision=HIGHEST, preferred_element_type=jnp.float32)
            pieces = []
            if k: pieces.append(r[:, :o])
            pieces.append(linv[m])
            if k < nblk - 1: pieces.append(r[:, o + NB:])
            rz = jnp.concatenate(pieces, axis=1)
            if k < nblk - 1:
                below = r[:, o + NB:]
                upd = lax.dot_general(below, rz, (((0,), (0,)), ((), ())), precision=HIGHEST, preferred_element_type=jnp.float32)
                old = o_ref[m, o + NB:, :]
                colid = lax.broadcasted_iota(jnp.int32, old.shape, 1)
                old = jnp.where((colid >= o) & (colid < o + NB), 0.0, old)
                o_ref[m, o + NB:, :] = old - upd
                colr = lax.broadcasted_iota(jnp.int32, rz.shape, 1)
                o_ref[m, o:o + NB, :] = jnp.where(colr < o + NB, rz, 0.0)
            else:
                o_ref[m, o:o + NB, :] = rz

def chol_inv(grams):
    return pl.pallas_call(chol_inv_kernel, out_shape=jax.ShapeDtypeStruct(grams.shape, jnp.float32),
        in_specs=[pl.BlockSpec(memory_space=pltpu.VMEM)], out_specs=pl.BlockSpec(memory_space=pltpu.VMEM),
        compiler_params=pltpu.CompilerParams(vmem_limit_bytes=48*1024*1024))(grams)


def local(inputs, preacts, cotangent, weights, left_stats, left_basis, right_stats, right_basis):
    row_share = left_stats.shape[1]
    col_share = left_stats.shape[2]
    full_rows, channels = weights.shape[1:]
    dp_index = lax.axis_index("dp")
    space_index = lax.axis_index("space")
    core = dp_index % 2
    complete = reduce_all(gradients(inputs[0, 0], preacts[0, 0, 0], cotangent[0, 0], weights[0]))

    row_block = lax.dynamic_slice_in_dim(complete, space_index * row_share, row_share, 1)
    col_block = lax.dynamic_slice_in_dim(complete, dp_index * col_share, col_share, 1)
    left_new = BETA * left_stats + (1.0 - BETA) * lax.dot_general(
        row_block, col_block, (((2,), (2,)), ((0,), (0,))), precision=HIGHEST
    )
    partial = lax.dot_general(left_new, left_basis, (((2,), (1,)), ((0,), (0,))), precision=HIGHEST)
    own, gram_left = gram_of_rows(jnp.pad(partial, ((0, 0), (0, PADDED - row_share), (0, 0))))

    pick = lambda x: lax.dynamic_index_in_dim(x, core, 0, keepdims=False)
    mine = pick(complete)
    gram_right = lax.dot_general(mine, mine, CONTRACT_ROWS, precision=HIGHEST)
    right_new = BETA * pick(right_stats) + (1.0 - BETA) * gram_right
    right_rows = jnp.dot(right_new, pick(right_basis), precision=HIGHEST)
    right_gram = lax.dot_general(right_rows, right_rows, CONTRACT_ROWS, precision=HIGHEST)
    inverses = chol_inv(jnp.stack([gram_left[:channels], right_gram]))
    basis_rows = math.sqrt(full_rows) * lax.dot_general(own, inverses[0], CONTRACT_COLS, precision=HIGHEST)
    turned = math.sqrt(channels) * lax.dot_general(right_rows, inverses[1], CONTRACT_COLS, precision=HIGHEST)
    spread_rows, right_both = spread(basis_rows, jnp.stack([right_new, turned]))
    return left_new, assemble(spread_rows, full_rows), right_both[:, 0], right_both[:, 1]


def solution(mesh):
    placed = (
        P("dp", None, "space", None, None),
        P(None, "dp", None, "space", None, None),
        P("dp", None, "space", None, None),
        P(),
        P(None, "space", "dp"),
        P(None, "dp", None),
        P(),
        P(),
    )
    return jax.shard_map(
        local,
        mesh=mesh,
        in_specs=placed,
        out_specs=(P(None, "space", "dp"), P(), P(), P()),
        check_vma=False,
    )
```

time: 782 us -> 292 us (0.37); the launches traced: 771 us -> 291 us
  waiting for transfers between devices: 502 us -> 0 us
  Pallas kernels: 36.5 us -> 245 us
  local copies, waits for them, and re-layouts: 117 us -> 23.9 us
  matrix products: 71.5 us -> 21.2 us
  other arithmetic: 16.5 us -> 0.13 us
  between operations: 14.7 us -> 0.84 us
  starting transfers between devices: 12.1 us -> 0 us
    psum x3 -> x0, waiting for transfers between devices: 378 us -> none  [the longest x1 161 us: local(): complete = lax.psum(gradient, ('dp', 'space'))]
    pallas_call x0 -> x5, Pallas kernels: none -> 213 us  [the longest x1 79.4 us: reduce_all(): pl.pallas_call(reduce_kernel, out_shape=jax.ShapeDtypeStruct(g.shape, jnp...]
    all_gather x2 -> x0, waiting for transfers between devices: 118 us -> none  [local(): basis_outs[i] = lax.all_gather(rows, 'space', axis=0, tiled=True)]
    dot_general x41 -> x6, matrix products: 69 us -> 19.9 us  [the longest x1 12.8 us: local(): gram_right = lax.dot_general(mine, mine, CONTRACT_ROWS, precision=HIGHEST)]
    slice x13 -> x0, local copies, waits for them, and re-layouts: 33.7 us -> none  [the longest x10 31.1 us: input_grad(): padded[:, :, 1 - row_step:1 - row_step + row_count, 1 - col_step:1 - col_...]
    reshape x9 -> x0, local copies, waits for them, and re-layouts: 32.8 us -> none  [input_grad(): shifted.reshape(-1, channels)]
    unnamed x75 -> x18, local copies, waits for them, and re-layouts: 7.42 us -> 22.3 us
    all_gather x2 -> x0, local copies, waits for them, and re-layouts: 12.6 us -> none  [local(): basis_outs[i] = lax.all_gather(rows, 'space', axis=0, tiled=True)]
  transfers between devices with their start and end apart: 9 -> 0, of which waited for: 7 -> 0; matrix products, arithmetic and copies ran while one was open for 5% -> 0% of each run, Pallas kernels for 0% -> 0%
where the time goes in v3:
time: 292 us; the launch traced here: 291 us
  Pallas kernels  245 us (84%)
  local copies, waits for them, and re-layouts  23.9 us (8%)
  matrix products  21.2 us (7%)
    pallas_call x1, Pallas kernels, reduce_all(): pl.pallas_call(reduce_kernel, out_shape=jax.ShapeDtypeStruct(g.shape, jnp...  79.4 us
    pallas_call x1, Pallas kernels, gradients(): pl.pallas_call(functools.partial(grads_kernel, remote, rows, cols), out_s...  45.8 us
    pallas_call x1, Pallas kernels, spread(): pl.pallas_call(spread_kernel, out_shape=(jax.ShapeDtypeStruct((2, 3, 1024...  42.7 us
    pallas_call x1, Pallas kernels, gram_of_rows(): pl.pallas_call(gram_kernel, out_shape=(jax.ShapeDtypeStruct((48, n), jnp....  33.9 us
    pallas_call x1, Pallas kernels, chol_inv(): pl.pallas_call(chol_inv_kernel, out_shape=jax.ShapeDtypeStruct(grams.shap...  32.5 us
    unnamed x18, local copies, waits for them, and re-layouts  22.3 us
    dot_general x1, matrix products, local(): gram_right = lax.dot_general(mine, mine, CONTRACT_ROWS, precision=HIGHEST)  12.8 us
    pallas_call x1, Pallas kernels, assemble(): pl.pallas_call(assemble_kernel, grid=(2, 8), out_shape=jax.ShapeDtypeStru...  10.8 us

profile of v3, /device:TPU:1, one launch (start us, length us, event | category | flops | bytes accessed | tf_op | source)
XLA Modules:
  0.0 291.1 jit_solution(7223324783420011043)
XLA Ops:
  0.6 0.0 copy-start
  0.7 1.9 copy.13
  2.6 2.5 copy.14
  5.1 2.5 copy.15
  7.6 4.0 %copy.16 = bf16[1,2880,320]{2,1,0:T(8,128)(2,1)} copy(bf16[1,2880,320]{1,2,0:T(8,128)(2,1)} %param.11) | data formatting | bytes 3686400 | tf_op args[3]
  11.6 0.0 copy-start.2
  11.6 1.4 copy-done.2
  13.0 45.8 %shard_map.111.g_ref = f32[2,2880,320]{2,1,0:T(8,128)} custom-call(bf16[1920,320]{1,0:T(8,128)(2,1)S(1)} %bitcast.39, bf16[1920,320]{1,0:T(8,128)(2,1)S(1)} %bitcast.40, bf16[1920,320]{1,0:T(8,128)(2,1)} %bitcast.42, bf16[2880,320]{1,0:T(8,128)(2,1)} %bitcast.41), custom_call_target="tpu_custom_call" | custom-call | tf_op jit(solution)/shard_map/pallas_call | solution.py:471
  58.8 0.0 copy-start.5
  58.8 79.4 %shard_map.112 = f32[2,2880,320]{2,1,0:T(8,128)} custom-call(f32[2,2880,320]{2,1,0:T(8,128)} %shard_map.111.g_ref), custom_call_target="tpu_custom_call" | custom-call | tf_op jit(solution)/shard_map/pallas_call | solution.py:206
  138.2 0.0 copy-done.5
  138.2 0.0 copy-start.3
  138.3 12.8 %fusion.9 = f32[320,320]{1,0:T(8,128)S(1)} fusion(f32[2,2880,320]{2,1,0:T(8,128)} %shard_map.112, s32[]{:T(128)S(6)} %select_n.23, f32[2,320,320]{2,1,0:T(8,128)S(1)} %copy-done.5), kind=kOutput, calls=%fused_computation.15 | convolution fusion | flops 3539251200 | bytes 5243904 | tf_op jit(solution)/shard_map/dot_general | solution.py:567
  151.1 0.0 copy-done.3
  151.1 3.0 %fusion.3 = f32[2,360,180]{1,2,0:T(8,128)S(1)} fusion(f32[2,2880,320]{2,1,0:T(8,128)} %shard_map.112, s32[]{:T(128)S(6)} %select_n.20, f32[2,360,180]{1,0,2:T(2,128)S(1)} %copy-done.3, s32[]{:T(128)S(6)} %select_n.21), kind=kOutput, calls=%fused_computation.4 | convolution fusion | flops 498052800 | bytes 2707976 | tf_op jit(solution)/shard_map/dot_general | solution.py:559
  154.0 0.0 copy-done
  154.1 0.0 copy-start.4
  154.1 1.1 fusion.15
  155.2 1.2 convolution_bitcast_fusion
  156.4 1.1 copy.20
  157.5 0.0 copy-done.4
  157.5 1.4 fusion.12
  158.9 0.1 pad.4.p_ref
  159.0 33.9 %shard_map.113 = (f32[48,320]{1,0:T(8,128)S(1)}, f32[384,320]{1,0:T(8,128)S(1)}) custom-call(f32[2,384,320]{2,1,0:T(8,128)S(1)} %pad.4.p_ref), custom_call_target="tpu_custom_call" | custom-call | tf_op jit(solution)/shard_map/pallas_call | solution.py:281
  193.0 0.1 pad_maximum_fusion.g_ref
  193.1 32.5 %shard_map.114 = f32[2,320,320]{2,1,0:T(8,128)S(1)} custom-call(f32[2,320,320]{2,1,0:T(8,128)S(1)} %pad_maximum_fusion.g_ref), custom_call_target="tpu_custom_call" | custom-call | tf_op jit(solution)/shard_map/pallas_call | solution.py:543
  225.5 1.1 fusion.4
  226.6 0.6 convolution_multiply_fusion.2.in_ref
  227.2 0.1 pad_maximum_fusion.1.x_ref
  227.3 42.7 %shard_map.115 = (f32[2,3,1024,320]{3,2,1,0:T(8,128)}, f32[2,2,320,320]{3,2,1,0:T(8,128)S(1)}) custom-call(f32[48,320]{1,0:T(8,128)S(1)} %convolution_multiply_fusion.2.in_ref, f32[2,320,320]{2,1,0:T(8,128)S(1)} %pad_maximum_fusion.1.x_ref), custom_call_target="tpu_custom_call" | custom-call | tf_op jit(solution)/shard_map/pallas_call | solution.py:348
  270.0 10.8 %shard_map.116 = f32[2,2880,320]{2,1,0:T(8,128)} custom-call(f32[2,3,1024,320]{3,2,1,0:T(8,128)} %get-tuple-element.10.in_ref), custom_call_target="tpu_custom_call" | custom-call | tf_op jit(solution)/shard_map/pallas_call | solution.py:377
  280.8 0.0 copy-start.1
  280.8 8.9 %copy.21 = f32[2,2880,320]{1,2,0:T(8,128)} copy(f32[2,2880,320]{2,1,0:T(8,128)} %shard_map.116) | data formatting | bytes 14745600
  289.7 1.4 slice_bitcast_fusion
  291.1 0.0 copy-done.1
  (1 shorter events, 0.0 us)
Async XLA Ops:
  0.6 153.4 %copy-start = (f32[2,320,320]{2,1,0:T(8,128)S(1)}, f32[2,320,320]{2,1,0:T(8,128)}, u32[]{:S(2)}) copy-start(f32[2,320,320]{2,1,0:T(8,128)} %param.15) | copy-start | bytes 2457604
  11.6 1.4 copy-start.2
  58.8 79.4 %copy-start.5 = (f32[2,320,320]{2,1,0:T(8,128)S(1)}, f32[2,320,320]{2,1,0:T(8,128)}, u32[]{:S(2)}) copy-start(f32[2,320,320]{2,1,0:T(8,128)} %param.14) | copy-start | bytes 2457604
  138.2 12.8 %copy-start.3 = (f32[2,360,180]{1,0,2:T(2,128)S(1)}, f32[2,360,180]{1,0,2:T(2,128)}, u32[]{:S(2)}) copy-start(f32[2,360,180]{1,0,2:T(2,128)} %param.12) | copy-start | bytes 1555204
  154.1 3.4 %copy-start.4 = (f32[2,180,320]{2,0,1:T(2,128)S(1)}, f32[2,180,320]{2,0,1:T(2,128)}, u32[]{:S(2)}) copy-start(f32[2,180,320]{2,0,1:T(2,128)} %param.13) | copy-start | bytes 1382404
  280.8 10.3 %copy-start.1 = (f32[2,320,320]{2,1,0:T(8,128)S(1)}, f32[2,320,320]{2,1,0:T(8,128)}, u32[]{:S(2)}) copy-start(f32[2,320,320]{2,1,0:T(8,128)} %param.15) | copy-start | bytes 2457604

commit v4 on v3

--- a/solution.py
+++ b/solution.py
@@ -214,7 +214,19 @@
     )(g)
 
 
-def gram_kernel(p_ref, own_ref, gram_ref, r0, r1, a, b, r2, c, r3, f, r4, send, recv):
+def view(ref, p, places, half=None):
+    row, size = 0, 1024
+    for c in places:
+        size = size // 4
+        row = row + c * size
+    if half is not None:
+        size = size // 2
+        row = row + half * size
+    return ref.at[p, pl.ds(pl.multiple_of(row, 16), size)]
+
+
+def gram_kernel(p_ref, g_ref, rs_ref, rb_ref, spread_ref, gram_ref, right_ref, rows_ref, rgram_ref,
+                r0, r1, a, own_ref, b, r2, c, r3, f, r4, acc, send, recv):
     core, place = coords()
     x, y, z = place
     quads = []
@@ -224,13 +236,40 @@
     partners += [device_at(core, to) for step, to in enumerate(quads, 1) if step // 2 and step % 2]
     greet(partners)
     out = Sender(send, recv)
-    out.start(p_ref.at[1 - core], r0, device_at(1 - core, place)).wait_recv()
+    first = out.start(p_ref.at[1 - core], r0, device_at(1 - core, place))
+    acc[...] = jnp.zeros_like(acc)
+
+    def right_body(i, carry):
+        x = g_ref[core, pl.ds(pl.multiple_of(i * 480, 16), 480), :]
+        high = x.astype(jnp.bfloat16)
+        low = (x - high.astype(jnp.float32)).astype(jnp.bfloat16)
+        acc[0] += lax.dot_general(high, high, CONTRACT_ROWS, preferred_element_type=jnp.float32)
+        acc[1] += lax.dot_general(high, low, CONTRACT_ROWS, preferred_element_type=jnp.float32)
+        return carry
+
+    lax.fori_loop(0, 6, right_body, 0)
+    cross = acc[1]
+    right = BETA * rs_ref[core] + (1.0 - BETA) * (acc[0] + (cross + cross.T))
+    right_ref[...] = right
+    first.wait_recv()
     add_rows(a, 0, [(r0, 0), (p_ref.at[core], 0)], PADDED, 96)
     block = lambda to: pl.multiple_of((to[0] * 2 + to[1] % 2) * 48, 16)
-    arrived([out.start(a.at[pl.ds(block(to), 48)], r1.at[k], device_at(core, to)) for k, to in enumerate(quads)])
+    quarter = [out.start(a.at[pl.ds(block(to), 48)], r1.at[k], device_at(core, to)) for k, to in enumerate(quads)]
+    right_rows = jnp.dot(right_ref[...], rb_ref[core], precision=HIGHEST, preferred_element_type=jnp.float32)
+    rows_ref[...] = right_rows
+    rgram_ref[...] = lax.dot_general(right_rows, right_rows, CONTRACT_ROWS, precision=HIGHEST,
+                                     preferred_element_type=jnp.float32)
+    arrived(quarter)
     add_rows(own_ref, 0, [(a, block(place))] + [(r1.at[k], 0) for k in range(7)], 48, 48)
     own = own_ref[...]
     n = own.shape[1]
+    spread3, spread2 = [], []
+    for p in range(3):
+        a1, a2, a3 = ORDERS[p]
+        row = pl.multiple_of((place[a2] * 4 + place[a3]) * 16, 16)
+        spread_ref[p, pl.ds(row, 16), :] = own_ref[pl.ds(16 * p, 16), :]
+        here = spread_ref.at[p, pl.ds(row, 16)]
+        spread3.append([out.start(here, here, device_at(core, to)) for to in peers(place, a3)])
     gram = lax.dot_general(own, own, CONTRACT_ROWS, precision=HIGHEST, preferred_element_type=jnp.float32)
     b[0, :, :] = gram[:128]
     b[1, :, :] = gram[128:256]
@@ -252,6 +291,11 @@
             for k, to in enumerate(peers(place, axis))
         ])
     for p in range(3):
+        arrived(spread3[p])
+        a2 = ORDERS[p][1]
+        here = spread_ref.at[p, pl.ds(pl.multiple_of(place[a2] * 64, 16), 64)]
+        spread2.append([out.start(here, here, device_at(core, to)) for to in peers(place, a2)])
+    for p in range(3):
         arrived(level2[p])
         add_rows(f.at[p], 0, [(c.at[p], place[ORDERS[p][1]] * 8)] + [(r3.at[p, k], 0) for k in range(3)], 8, 8)
         axis = ORDERS[p][2]
@@ -272,116 +316,24 @@
         gather1.append([out.start(here, here, device_at(core, to)) for to in peers(place, axis)])
     for p in range(3):
         arrived(gather1[p])
+        arrived(spread2[p])
     out.finish()
 
 
-def gram_of_rows(partial):
+def gram_of_rows(partial, complete, right_stats, right_basis):
     n = partial.shape[-1]
     vm = lambda *s: pltpu.VMEM(s + (n,), jnp.float32)
+    square = jax.ShapeDtypeStruct((n, n), jnp.float32)
     return pl.pallas_call(
         gram_kernel,
-        out_shape=(jax.ShapeDtypeStruct((48, n), jnp.float32), jax.ShapeDtypeStruct((PADDED, n), jnp.float32)),
-        in_specs=[pl.BlockSpec(memory_space=pltpu.VMEM)],
-        out_specs=(pl.BlockSpec(memory_space=pltpu.VMEM),) * 2,
-        scratch_shapes=[vm(PADDED), vm(7, 48), vm(PADDED), vm(3, 128), vm(3, 3, 32), vm(3, 32), vm(3, 3, 8), vm(3, 8),
-                        vm(3, 3, 8), pltpu.SemaphoreType.DMA((53,)), pltpu.SemaphoreType.DMA((53,))],
+        out_shape=(jax.ShapeDtypeStruct((3, 256, n), jnp.float32), jax.ShapeDtypeStruct((PADDED, n), jnp.float32),
+                   square, square, square),
+        in_specs=[pl.BlockSpec(memory_space=pltpu.VMEM)] * 4,
+        out_specs=(pl.BlockSpec(memory_space=pltpu.VMEM),) * 5,
+        scratch_shapes=[vm(PADDED), vm(7, 48), vm(PADDED), vm(48), vm(3, 128), vm(3, 3, 32), vm(3, 32), vm(3, 3, 8),
+                        vm(3, 8), vm(3, 3, 8), vm(2, n), pltpu.SemaphoreType.DMA((71,)), pltpu.SemaphoreType.DMA((71,))],
         compiler_params=kernel_params(1),
-    )(partial)
-
-
-def spread_kernel(in_ref, x_ref, o_ref, y_ref, send, recv):
-    core, place = coords()
-    greet(all_partners(core, place))
-    sibling = device_at(1 - core, place)
-    out = Sender(send, recv)
-    last = [out.start(x_ref, y_ref.at[core], sibling)]
-    y_ref[core] = x_ref[...]
-
-    def view(p, places, half=None):
-        row, size = 0, 1024
-        for c in places:
-            size = size // 4
-            row = row + c * size
-        if half is not None:
-            size = size // 2
-            row = row + half * size
-        return o_ref.at[core, p, pl.ds(pl.multiple_of(row, 16), size)]
-
-    pending, gather1a, gather1b = [], {}, {}
-    for p in range(3):
-        a1, a2, a3 = ORDERS[p]
-        here = view(p, (place[a1], place[a2], place[a3]))
-        here[...] = in_ref[pl.ds(16 * p, 16), :]
-        pending.append([out.start(here, here, device_at(core, to)) for to in peers(place, a3)])
-    for p in range(3):
-        arrived(pending[p])
-        a1, a2, a3 = ORDERS[p]
-        here = view(p, (place[a1], place[a2]))
-        pending[p] = [out.start(here, here, device_at(core, to)) for to in peers(place, a2)]
-    for p in range(3):
-        arrived(pending[p])
-        axis = ORDERS[p][0]
-        x = place[axis]
-        for half in range(2):
-            near, far = ring_pairs(half)
-            here = view(p, (x,), half)
-            gather1a[p, half] = out.start(here, here, device_at(core, moved_to(place, axis, far(x))))
-            gather1b[p, half] = [out.start(here, here, device_at(core, moved_to(place, axis, near(x))))]
-    for p in range(3):
-        axis = ORDERS[p][0]
-        x = place[axis]
-        for half in range(2):
-            near, far = ring_pairs(half)
-            gather1a[p, half].wait_recv()
-            here = view(p, (far(x),), half)
-            gather1b[p, half].append(out.start(here, here, device_at(core, moved_to(place, axis, near(x)))))
-    for p in range(3):
-        for half in range(2):
-            arrived(gather1b[p, half])
-        last.append(out.start(o_ref.at[core, p], o_ref.at[core, p], sibling))
-    arrived(last)
-    out.finish()
-
-
-def spread(rows, extra):
-    n = rows.shape[1]
-    return pl.pallas_call(
-        spread_kernel,
-        out_shape=(jax.ShapeDtypeStruct((2, 3, 1024, n), jnp.float32),
-                   jax.ShapeDtypeStruct((2,) + extra.shape, jnp.float32)),
-        in_specs=[pl.BlockSpec(memory_space=pltpu.VMEM)] * 2,
-        out_specs=(pl.BlockSpec(memory_space=pltpu.VMEM),) * 2,
-        scratch_shapes=[pltpu.SemaphoreType.DMA((40,)), pltpu.SemaphoreType.DMA((40,))],
-        compiler_params=kernel_params(2),
-    )(rows, extra)
-
-
-def assemble_kernel(in_ref, o_ref):
-    layer, block = pl.program_id(0), pl.program_id(1)
-    z, y_high = block // 2, block % 2
-    for q in range(8):
-        place = (q // 2, y_high * 2 + q % 2, z)
-        for p in range(3):
-            row = 48 * q + 16 * p
-            size = min(16, o_ref.shape[1] - row)
-            if size <= 0:
-                continue
-            a1, a2, a3 = ORDERS[p]
-            src = pl.multiple_of(((place[a1] * 4 + place[a2]) * 4 + place[a3]) * 16, 16)
-            o_ref[0, row:row + size, :] = in_ref[layer, p, pl.ds(src, size), :]
-
-
-def assemble(spread_out, full_rows):
-    n = spread_out.shape[-1]
-    share = full_rows // 8
-    return pl.pallas_call(
-        assemble_kernel,
-        grid=(2, 8),
-        out_shape=jax.ShapeDtypeStruct((2, full_rows, n), jnp.float32),
-        in_specs=[pl.BlockSpec(memory_space=pltpu.VMEM)],
-        out_specs=pl.BlockSpec((1, share, n), lambda i, j: (i, j, 0)),
-        compiler_params=kernel_params(),
-    )(spread_out)
+    )(partial, complete, right_stats, right_basis)
 
 
 def three_wide(x):
@@ -480,69 +432,180 @@
 
 NB = 64
 
+
 def diag_inverse(blocks):
     n = NB
+    shape = (8, 2 * n)
     row = lax.broadcasted_iota(jnp.int32, (n, 2 * n), 0)
     col = lax.broadcasted_iota(jnp.int32, (n, 2 * n), 1)
     eye = jnp.where(row + n == col, 1.0, 0.0).astype(jnp.float32)
+    sub = lax.broadcasted_iota(jnp.int32, shape, 0)
     tiles = []
     for b in blocks:
         x = jnp.concatenate([b, jnp.zeros((n, n), jnp.float32)], axis=1) + eye
         tiles.append([x[8 * t:8 * t + 8] for t in range(n // 8)])
-    sub = lax.broadcasted_iota(jnp.int32, (8, 2 * n), 0)
     scales = [[None] * (n // 8) for _ in blocks]
-    for j in range(n):
-        tj, sj = j // 8, j % 8
+    for tj in range(n // 8):
+        steps = [[] for _ in blocks]
         for m in range(len(blocks)):
-            x = tiles[m]
-            pivot_row = x[tj][sj:sj + 1, :]
-            cb = jnp.broadcast_to(x[tj][:, j:j + 1], (8, 2 * n))
-            d = cb[sj:sj + 1, :]
-            rs = lax.rsqrt(d)
-            scales[m][tj] = jnp.where(sub == sj, rs, scales[m][tj] if sj else 0.0)
-            scaled = pivot_row * (rs * rs)
-            if sj < 7:
-                x[tj] = x[tj] - jnp.where(sub > sj, cb, 0.0) * scaled
+            x = tiles[m][tj]
+            c = [jnp.broadcast_to(x[:, 8 * tj + k:8 * tj + k + 1], shape) for k in range(8)]
+            scale = jnp.zeros(shape, jnp.float32)
+            for k in range(8):
+                rs = lax.rsqrt(jnp.broadcast_to(c[k][k:k + 1, :], shape))
+                inv = rs * rs
+                scale = jnp.where(sub == k, rs, scale)
+                scaled = jnp.broadcast_to(x[k:k + 1, :], shape) * inv
+                factors = []
+                for kk in range(k + 1, 8):
+                    factor = jnp.broadcast_to(c[kk][k:k + 1, :], shape) * inv
+                    c[kk] = c[kk] - c[k] * factor
+                    factors.append(factor)
+                if k < 7:
+                    x = x - jnp.where(sub > k, c[k], 0.0) * scaled
+                steps[m].append((scaled, factors))
+            tiles[m][tj] = x
+            scales[m][tj] = scale
+        for m in range(len(blocks)):
             for t in range(tj + 1, n // 8):
-                x[t] = x[t] - jnp.broadcast_to(x[t][:, j:j + 1], (8, 2 * n)) * scaled
+                x = tiles[m][t]
+                c = [jnp.broadcast_to(x[:, 8 * tj + k:8 * tj + k + 1], shape) for k in range(8)]
+                for k in range(8):
+                    scaled, factors = steps[m][k]
+                    for kk in range(k + 1, 8):
+                        c[kk] = c[kk] - c[k] * factors[kk - k - 1]
+                    x = x - c[k] * scaled
+                tiles[m][t] = x
     out = []
     for m in range(len(blocks)):
         w = jnp.concatenate([tiles[m][t] * scales[m][t] for t in range(n // 8)], axis=0)
         out.append(w[:, n:])
     return out
 
-def chol_inv_kernel(g_ref, o_ref):
-    nm, size, _ = g_ref.shape
-    o_ref[...] = g_ref[...]
-    nblk = size // NB
-    for k in range(nblk):
-        o = k * NB
-        linv = diag_inverse([o_ref[m, o:o + NB, o:o + NB] for m in range(nm)])
-        for m in range(nm):
-            parts = []
-            prow = o_ref[m, o:o + NB, :]
-            r = jnp.dot(linv[m], prow, precision=HIGHEST, preferred_element_type=jnp.float32)
-            pieces = []
-            if k: pieces.append(r[:, :o])
-            pieces.append(linv[m])
-            if k < nblk - 1: pieces.append(r[:, o + NB:])
-            rz = jnp.concatenate(pieces, axis=1)
-            if k < nblk - 1:
-                below = r[:, o + NB:]
-                upd = lax.dot_general(below, rz, (((0,), (0,)), ((), ())), precision=HIGHEST, preferred_element_type=jnp.float32)
-                old = o_ref[m, o + NB:, :]
-                colid = lax.broadcasted_iota(jnp.int32, old.shape, 1)
-                old = jnp.where((colid >= o) & (colid < o + NB), 0.0, old)
-                o_ref[m, o + NB:, :] = old - upd
-                colr = lax.broadcasted_iota(jnp.int32, rz.shape, 1)
-                o_ref[m, o:o + NB, :] = jnp.where(colr < o + NB, rz, 0.0)
-            else:
-                o_ref[m, o:o + NB, :] = rz
-
-def chol_inv(grams):
-    return pl.pallas_call(chol_inv_kernel, out_shape=jax.ShapeDtypeStruct(grams.shape, jnp.float32),
-        in_specs=[pl.BlockSpec(memory_space=pltpu.VMEM)], out_specs=pl.BlockSpec(memory_space=pltpu.VMEM),
-        compiler_params=pltpu.CompilerParams(vmem_limit_bytes=48*1024*1024))(grams)
+
+def factor_step(m_ref, k):
+    count, size, _ = m_ref.shape
+    o = k * NB
+    linv = diag_inverse([m_ref[m, o:o + NB, o:o + NB] for m in range(count)])
+    for m in range(count):
+        r = jnp.dot(linv[m], m_ref[m, o:o + NB, :], precision=HIGHEST, preferred_element_type=jnp.float32)
+        pieces = ([r[:, :o]] if k else []) + [linv[m]] + ([r[:, o + NB:]] if o + NB < size else [])
+        rz = jnp.concatenate(pieces, axis=1)
+        if o + NB == size:
+            m_ref[m, o:, :] = rz
+            continue
+        change = lax.dot_general(r[:, o + NB:], rz, CONTRACT_ROWS, precision=HIGHEST, preferred_element_type=jnp.float32)
+        old = m_ref[m, o + NB:, :]
+        col = lax.broadcasted_iota(jnp.int32, old.shape, 1)
+        m_ref[m, o + NB:, :] = jnp.where((col >= o) & (col < o + NB), 0.0, old) - change
+        col = lax.broadcasted_iota(jnp.int32, rz.shape, 1)
+        m_ref[m, o:o + NB, :] = jnp.where(col < o + NB, rz, 0.0)
+
+
+def factor_kernel(s_ref, gram_ref, right_ref, rows_ref, rgram_ref, o_ref, y_ref, m_ref, send, recv):
+    core, place = coords()
+    n = rgram_ref.shape[0]
+    greet(all_partners(core, place))
+    sibling = device_at(1 - core, place)
+    out = Sender(send, recv)
+    mine = o_ref.at[core]
+    y_ref[core, 0] = right_ref[...]
+    last = [out.start(y_ref.at[core, 0], y_ref.at[core, 0], sibling)]
+    gather1a, gather1b = {}, {}
+    for p in range(3):
+        axis = ORDERS[p][0]
+        x = place[axis]
+        mine[p, pl.ds(pl.multiple_of(x * 256, 16), 256), :] = s_ref[p]
+        for half in range(2):
+            near, far = ring_pairs(half)
+            here = view(mine, p, (x,), half)
+            gather1a[p, half] = out.start(here, here, device_at(core, moved_to(place, axis, far(x))))
+            gather1b[p, half] = [out.start(here, here, device_at(core, moved_to(place, axis, near(x))))]
+    m_ref[0] = gram_ref[:n, :]
+    m_ref[1] = rgram_ref[...]
+    steps = n // NB
+    for k in range(2):
+        factor_step(m_ref, k)
+    for p in range(3):
+        axis = ORDERS[p][0]
+        x = place[axis]
+        for half in range(2):
+            near, far = ring_pairs(half)
+            gather1a[p, half].wait_recv()
+            here = view(mine, p, (far(x),), half)
+            gather1b[p, half].append(out.start(here, here, device_at(core, moved_to(place, axis, near(x)))))
+    for k in range(2, steps - 1):
+        factor_step(m_ref, k)
+    for p in range(3):
+        for half in range(2):
+            arrived(gather1b[p, half])
+        last.append(out.start(mine.at[p], mine.at[p], sibling))
+    factor_step(m_ref, steps - 1)
+    y_ref[core, 1] = m_ref[0]
+    last.append(out.start(y_ref.at[core, 1], y_ref.at[core, 1], sibling))
+    y_ref[core, 2] = math.sqrt(n) * lax.dot_general(
+        rows_ref[...], m_ref[1], CONTRACT_COLS, precision=HIGHEST, preferred_element_type=jnp.float32
+    )
+    last.append(out.start(y_ref.at[core, 2], y_ref.at[core, 2], sibling))
+    arrived(last)
+    out.finish()
+
+
+def factor(*pieces):
+    n = pieces[0].shape[-1]
+    return pl.pallas_call(
+        factor_kernel,
+        out_shape=(jax.ShapeDtypeStruct((2, 3, 1024, n), jnp.float32), jax.ShapeDtypeStruct((2, 3, n, n), jnp.float32)),
+        in_specs=[pl.BlockSpec(memory_space=pltpu.VMEM)] * 5,
+        out_specs=(pl.BlockSpec(memory_space=pltpu.VMEM),) * 2,
+        scratch_shapes=[pltpu.VMEM((2, n, n), jnp.float32), pltpu.SemaphoreType.DMA((24,)), pltpu.SemaphoreType.DMA((24,))],
+        compiler_params=kernel_params(2),
+    )(*pieces)
+
+
+def basis_kernel(full_rows, in_ref, y_ref, o_ref, dense):
+    layer = pl.program_id(0)
+    share = full_rows // 8
+
+    def place_rows(block, carry):
+        z, y_high = block // 2, block % 2
+        for q in range(8):
+            place = (q // 2, y_high * 2 + q % 2, z)
+            for p in range(3):
+                row = 48 * q + 16 * p
+                size = min(16, share - row)
+                if size <= 0:
+                    continue
+                a1, a2, a3 = ORDERS[p]
+                src = pl.multiple_of(((place[a1] * 4 + place[a2]) * 4 + place[a3]) * 16, 16)
+                dense[pl.ds(pl.multiple_of(block * share + row, 8), size), :] = in_ref[layer, p, pl.ds(src, size), :]
+        return carry
+
+    lax.fori_loop(0, 8, place_rows, 0)
+
+    def halves(x):
+        high = x.astype(jnp.bfloat16)
+        return high, (x - high.astype(jnp.float32)).astype(jnp.bfloat16)
+
+    times = lambda x, y: lax.dot_general(x, y, CONTRACT_COLS, preferred_element_type=jnp.float32)
+    l_high, l_low = halves(y_ref[layer, 1] * math.sqrt(full_rows))
+    for start in range(0, full_rows, 768):
+        size = min(768, full_rows - start)
+        high, low = halves(dense[start:start + size, :])
+        o_ref[0, :, start:start + size] = times(l_high, high) + (times(l_high, low) + times(l_low, high))
+
+
+def basis_of(spread_rows, both, full_rows):
+    n = spread_rows.shape[-1]
+    return pl.pallas_call(
+        functools.partial(basis_kernel, full_rows),
+        grid=(2,),
+        out_shape=jax.ShapeDtypeStruct((2, n, full_rows), jnp.float32),
+        in_specs=[pl.BlockSpec(memory_space=pltpu.VMEM)] * 2,
+        out_specs=pl.BlockSpec((1, n, full_rows), lambda i: (i, 0, 0)),
+        scratch_shapes=[pltpu.VMEM((full_rows, n), jnp.float32)],
+        compiler_params=kernel_params(),
+    )(spread_rows, both)
 
 
 def local(inputs, preacts, cotangent, weights, left_stats, left_basis, right_stats, right_basis):
@@ -551,7 +614,6 @@
     full_rows, channels = weights.shape[1:]
     dp_index = lax.axis_index("dp")
     space_index = lax.axis_index("space")
-    core = dp_index % 2
     complete = reduce_all(gradients(inputs[0, 0], preacts[0, 0, 0], cotangent[0, 0], weights[0]))
 
     row_block = lax.dynamic_slice_in_dim(complete, space_index * row_share, row_share, 1)
@@ -560,19 +622,10 @@
         row_block, col_block, (((2,), (2,)), ((0,), (0,))), precision=HIGHEST
     )
     partial = lax.dot_general(left_new, left_basis, (((2,), (1,)), ((0,), (0,))), precision=HIGHEST)
-    own, gram_left = gram_of_rows(jnp.pad(partial, ((0, 0), (0, PADDED - row_share), (0, 0))))
-
-    pick = lambda x: lax.dynamic_index_in_dim(x, core, 0, keepdims=False)
-    mine = pick(complete)
-    gram_right = lax.dot_general(mine, mine, CONTRACT_ROWS, precision=HIGHEST)
-    right_new = BETA * pick(right_stats) + (1.0 - BETA) * gram_right
-    right_rows = jnp.dot(right_new, pick(right_basis), precision=HIGHEST)
-    right_gram = lax.dot_general(right_rows, right_rows, CONTRACT_ROWS, precision=HIGHEST)
-    inverses = chol_inv(jnp.stack([gram_left[:channels], right_gram]))
-    basis_rows = math.sqrt(full_rows) * lax.dot_general(own, inverses[0], CONTRACT_COLS, precision=HIGHEST)
-    turned = math.sqrt(channels) * lax.dot_general(right_rows, inverses[1], CONTRACT_COLS, precision=HIGHEST)
-    spread_rows, right_both = spread(basis_rows, jnp.stack([right_new, turned]))
-    return left_new, assemble(spread_rows, full_rows), right_both[:, 0], right_both[:, 1]
+    padded = jnp.pad(partial, ((0, 0), (0, PADDED - row_share), (0, 0)))
+    spread_rows, both = factor(*gram_of_rows(padded, complete, right_stats, right_basis))
+    basis_out = jnp.swapaxes(basis_of(spread_rows, both, full_rows), 1, 2)
+    return left_new, basis_out, both[:, 0], both[:, 2]
 
 
 def solution(mesh):

time: 292 us -> 239 us (0.82)
  Pallas kernels: 245 us -> 216 us
  matrix products: 21.2 us -> 4.4 us
  local copies, waits for them, and re-layouts: 23.9 us -> 17.7 us
    pallas_call x4 -> x3, Pallas kernels: 120 us -> 90.9 us  [the longest x1 41.4 us: gram_of_rows(): pl.pallas_call(gram_kernel, out_shape=(jax.ShapeDtypeStruct((3, 256, n),...]
    dot_general x5 -> x0, matrix products: 16.8 us -> none  [the longest x1 12.8 us: local(): gram_right = lax.dot_general(mine, mine, CONTRACT_ROWS, precision=HIGHEST)]
    unnamed x18 -> x17, local copies, waits for them, and re-layouts: 22.3 us -> 15.2 us
where the time goes in v4:
time: 239 us
  Pallas kernels  216 us (90%)
  local copies, waits for them, and re-layouts  17.7 us (7%)
  matrix products  4.4 us (2%)
    pallas_call x1, Pallas kernels, reduce_all(): pl.pallas_call(reduce_kernel, out_shape=jax.ShapeDtypeStruct(g.shape, jnp...  79.5 us
    pallas_call x1, Pallas kernels, gradients(): pl.pallas_call(functools.partial(grads_kernel, remote, rows, cols), out_s...  45.7 us
    pallas_call x1, Pallas kernels, gram_of_rows(): pl.pallas_call(gram_kernel, out_shape=(jax.ShapeDtypeStruct((3, 256, n),...  41.4 us
    pallas_call x1, Pallas kernels, factor(): pl.pallas_call(factor_kernel, out_shape=(jax.ShapeDtypeStruct((2, 3, 1024...  36.1 us
    unnamed x17, local copies, waits for them, and re-layouts  15.2 us
    pallas_call x1, Pallas kernels, basis_of(): pl.pallas_call(functools.partial(basis_kernel, full_rows), grid=(2,), out...  13.4 us

profile of v4, /device:TPU:1, one launch (start us, length us, event | category | flops | bytes accessed | tf_op | source)
XLA Modules:
  0.0 239.0 jit_solution(6113946313601647071)
XLA Ops:
  0.6 0.0 copy-start
  0.7 1.9 copy.13
  2.5 1.8 copy.14
  4.4 2.5 %copy.15 = bf16[1,1,8,240,320]{4,3,2,1,0:T(8,128)(2,1)} copy(bf16[1,1,8,240,320]{3,4,2,1,0:T(8,128)(2,1)} %param.10) | data formatting | bytes 2457600 | tf_op args[2]
  6.9 4.0 %copy.16 = bf16[1,2880,320]{2,1,0:T(8,128)(2,1)} copy(bf16[1,2880,320]{1,2,0:T(8,128)(2,1)} %param.11) | data formatting | bytes 3686400 | tf_op args[3]
  10.9 45.7 %shard_map.111.g_ref = f32[2,2880,320]{2,1,0:T(8,128)} custom-call(bf16[1920,320]{1,0:T(8,128)(2,1)S(1)} %bitcast.10, bf16[1920,320]{1,0:T(8,128)(2,1)S(1)} %bitcast.11, bf16[1920,320]{1,0:T(8,128)(2,1)} %bitcast.14, bf16[2880,320]{1,0:T(8,128)(2,1)} %bitcast.12), custom_call_target="tpu_custom_call" | custom-call | tf_op jit(solution)/shard_map/pallas_call | solution.py:423
  56.6 0.0 copy-start.5
  56.6 79.5 %shard_map.112.g_ref = f32[2,2880,320]{2,1,0:T(8,128)} custom-call(f32[2,2880,320]{2,1,0:T(8,128)} %shard_map.111.g_ref), custom_call_target="tpu_custom_call" | custom-call | tf_op jit(solution)/shard_map/pallas_call | solution.py:206
  136.1 0.0 copy-done.5
  136.2 3.0 %fusion = f32[2,360,180]{1,2,0:T(8,128)S(1)} fusion(f32[2,2880,320]{2,1,0:T(8,128)} %shard_map.112.g_ref, s32[]{:T(128)S(6)} %select_n.6, f32[2,360,180]{1,0,2:T(2,128)S(1)} %copy-done.5, s32[]{:T(128)S(6)} %select_n.7), kind=kOutput, calls=%fused_computation.1 | convolution fusion | flops 498052800 | bytes 2707976 | tf_op jit(solution)/shard_map/dot_general | solution.py:621
  139.1 1.1 copy.20
  140.2 0.0 copy-done
  140.2 1.4 fusion.2
  141.7 0.0 copy-start.3
  141.7 0.0 copy-start.4
  141.7 1.1 pad.4.p_ref
  142.8 0.5 copy-done.3
  143.3 0.3 copy-done.4
  143.6 41.4 %shard_map.113 = (f32[3,256,320]{2,1,0:T(8,128)}, f32[384,320]{1,0:T(8,128)S(1)}, f32[320,320]{1,0:T(8,128)S(1)}, f32[320,320]{1,0:T(8,128)S(1)}, f32[320,320]{1,0:T(8,128)S(1)}) custom-call(f32[2,384,320]{2,1,0:T(8,128)} %pad.4.p_ref, f32[2,2880,320]{2,1,0:T(8,128)} %shard_map.112.g_ref, f32[2,320,320]{2,1,0:T(8,128)S(1)} %copy-done.3, ...), custom_call_target="tpu_custom_call" | custom-call | tf_op jit(solution)/shard_map/pallas_call | solution.py:327
  185.0 0.0 copy-start.2
  185.1 1.3 copy-done.2
  186.3 36.1 %shard_map.114 = (f32[2,3,1024,320]{3,2,1,0:T(8,128)}, f32[2,3,320,320]{3,2,1,0:T(8,128)}) custom-call(f32[3,256,320]{2,1,0:T(8,128)S(1)} %copy-done.2, f32[384,320]{1,0:T(8,128)S(1)} %get-tuple-element.12.gram_ref, f32[320,320]{1,0:T(8,128)S(1)} %get-tuple-element.13.right_ref, f32[320,320]{1,0:T(8,128)S(1)} %get-tuple-element.14.rows_ref, ...), custom_call_target="tpu_custom_call" | custom-call | tf_op jit(solution)/shard_map/pallas_call | solution.py:556
  222.4 0.0 copy-start.1
  222.4 1.8 copy-done.1
  224.2 13.4 %shard_map.115 = f32[2,320,2880]{2,1,0:T(8,128)} custom-call(f32[2,3,1024,320]{3,2,1,0:T(8,128)} %get-tuple-element.16.in_ref, f32[2,3,320,320]{3,2,1,0:T(8,128)S(1)} %copy-done.1), custom_call_target="tpu_custom_call" | custom-call | tf_op jit(solution)/shard_map/pallas_call | solution.py:600
  237.6 1.4 slice_bitcast_fusion
Async XLA Ops:
  0.6 139.6 %copy-start = (f32[2,180,320]{2,0,1:T(2,128)S(1)}, f32[2,180,320]{2,0,1:T(2,128)}, u32[]{:S(2)}) copy-start(f32[2,180,320]{2,0,1:T(2,128)} %param.13) | copy-start | bytes 1382404
  56.6 79.5 %copy-start.5 = (f32[2,360,180]{1,0,2:T(2,128)S(1)}, f32[2,360,180]{1,0,2:T(2,128)}, u32[]{:S(2)}) copy-start(f32[2,360,180]{1,0,2:T(2,128)} %param.12) | copy-start | bytes 1555204
  141.7 1.6 copy-start.3
  141.7 1.9 copy-start.4
  185.0 1.3 copy-start.2
  222.4 1.8 copy-start.1

commit v5 on v4

--- a/solution.py
+++ b/solution.py
@@ -247,18 +247,12 @@
         acc[1] += lax.dot_general(high, low, CONTRACT_ROWS, preferred_element_type=jnp.float32)
         return carry
 
-    lax.fori_loop(0, 6, right_body, 0)
-    cross = acc[1]
-    right = BETA * rs_ref[core] + (1.0 - BETA) * (acc[0] + (cross + cross.T))
-    right_ref[...] = right
+    lax.fori_loop(0, 2, right_body, 0)
     first.wait_recv()
     add_rows(a, 0, [(r0, 0), (p_ref.at[core], 0)], PADDED, 96)
     block = lambda to: pl.multiple_of((to[0] * 2 + to[1] % 2) * 48, 16)
     quarter = [out.start(a.at[pl.ds(block(to), 48)], r1.at[k], device_at(core, to)) for k, to in enumerate(quads)]
-    right_rows = jnp.dot(right_ref[...], rb_ref[core], precision=HIGHEST, preferred_element_type=jnp.float32)
-    rows_ref[...] = right_rows
-    rgram_ref[...] = lax.dot_general(right_rows, right_rows, CONTRACT_ROWS, precision=HIGHEST,
-                                     preferred_element_type=jnp.float32)
+    lax.fori_loop(2, 4, right_body, 0)
     arrived(quarter)
     add_rows(own_ref, 0, [(a, block(place))] + [(r1.at[k], 0) for k in range(7)], 48, 48)
     own = own_ref[...]
@@ -282,6 +276,7 @@
             out.start(b.at[p, pl.ds(pl.multiple_of(to[axis] * 32, 8), 32)], r2.at[p, k], device_at(core, to))
             for k, to in enumerate(peers(place, axis))
         ])
+    lax.fori_loop(4, 5, right_body, 0)
     for p in range(3):
         arrived(level1[p])
         add_rows(c.at[p], 0, [(b.at[p], place[ORDERS[p][0]] * 32)] + [(r2.at[p, k], 0) for k in range(3)], 32, 32)
@@ -295,6 +290,9 @@
         a2 = ORDERS[p][1]
         here = spread_ref.at[p, pl.ds(pl.multiple_of(place[a2] * 64, 16), 64)]
         spread2.append([out.start(here, here, device_at(core, to)) for to in peers(place, a2)])
+    lax.fori_loop(5, 6, right_body, 0)
+    cross = acc[1]
+    right_ref[...] = BETA * rs_ref[core] + (1.0 - BETA) * (acc[0] + (cross + cross.T))
     for p in range(3):
         arrived(level2[p])
         add_rows(f.at[p], 0, [(c.at[p], place[ORDERS[p][1]] * 8)] + [(r3.at[p, k], 0) for k in range(3)], 8, 8)
@@ -302,6 +300,8 @@
         level3.append([
             out.start(f.at[p], r4.at[p, k], device_at(core, to)) for k, to in enumerate(peers(place, axis))
         ])
+    right_rows = jnp.dot(right_ref[...], rb_ref[core], precision=HIGHEST, preferred_element_type=jnp.float32)
+    rows_ref[...] = right_rows
     for p in range(3):
         arrived(level3[p])
         axis = ORDERS[p][1]
@@ -309,6 +309,8 @@
         add_rows(gram_ref, row, [(f.at[p], 0)] + [(r4.at[p, k], 0) for k in range(3)], 8, 8)
         here = gram_ref.at[pl.ds(row, 8)]
         gather2.append([out.start(here, here, device_at(core, to)) for to in peers(place, axis)])
+    rgram_ref[...] = lax.dot_general(right_rows, right_rows, CONTRACT_ROWS, precision=HIGHEST,
+                                     preferred_element_type=jnp.float32)
     for p in range(3):
         arrived(gather2[p])
         axis = ORDERS[p][0]
@@ -336,98 +338,121 @@
     )(partial, complete, right_stats, right_basis)
 
 
-def three_wide(x):
-    cols = x.shape[0]
-    col = lax.broadcasted_iota(jnp.int32, x.shape, 0)
-    before = jnp.where(col == 0, 0.0, pltpu.roll(x, 1, 0))
-    after = jnp.where(col == cols - 1, 0.0, pltpu.roll(x, cols - 1, 0))
-    return jnp.concatenate([v.astype(jnp.bfloat16) for v in (before, x, after)], axis=1)
-
-def grads_kernel(remote, rows, cols, a_ref, v_ref, g_ref, w_ref, o_ref, rims, wide, wide_g, back, g_t, w_t, send, recv):
-    n = a_ref.shape[1]
+LANES = 256
+
+def widened(x):
+    return jnp.concatenate([x, jnp.zeros((x.shape[0], LANES - x.shape[1]), x.dtype)], axis=1)
+
+def put_taps(x, dst, r):
+    n = x.shape[0]
+    x = widened(x)
+    lanes = pl.ds(pl.multiple_of(r * LANES, LANES), LANES)
+    for i, v in enumerate((pltpu.roll(x, 1, 1), x, pltpu.roll(x, LANES - 1, 1))):
+        dst[pl.ds(i * n, n), lanes] = v.astype(jnp.bfloat16)
+
+def grads_kernel(remote, a_ref, v_ref, g_ref, w_ref, o_ref, rims, wide_v, wide_a, wide_g, back, g_n, w_l, send, recv):
+    rows, n, cols = a_ref.shape
+    span = rows * LANES
     copies = []
     if remote:
         me = lax.axis_index("space")
         up, down = (me + 7) % 8, (me + 1) % 8
         greet([{"space": up}, {"space": down}])
-        for i, ref in enumerate((g_ref, v_ref, a_ref)):
-            for side, (first, to) in enumerate((((rows - 1) * cols, down), (0, up))):
-                copy = pltpu.make_async_remote_copy(src_ref=ref.at[pl.ds(first, cols)], dst_ref=rims.at[i, side],
+        for i, ref in enumerate((g_ref, a_ref)):
+            for side, (first, to) in enumerate(((rows - 1, down), (0, up))):
+                copy = pltpu.make_async_remote_copy(
+                    src_ref=ref.at[first], dst_ref=rims.at[i, side],
                     send_sem=send.at[2 * i + side], recv_sem=recv.at[2 * i + side],
-                    device_id={"space": to}, device_id_type=pl.DeviceIdType.MESH)
+                    device_id={"space": to}, device_id_type=pl.DeviceIdType.MESH,
+                )
                 copy.start()
                 copies.append(copy)
         has = (me > 0, me < 7)
     else:
-        has = (True, True)
+        has = (False, False)
     same = lambda x: x
     silu = lambda x: (x * jax.nn.sigmoid(x)).astype(jnp.bfloat16).astype(jnp.float32)
-    def widen_rows(ref, dst, change):
+
+    def widen_rows(ref, dst, change, offset):
         def body(r, carry):
-            x = change(ref[pl.ds(pl.multiple_of(r * cols, 16), cols), :].astype(jnp.float32))
-            dst[pl.ds(pl.multiple_of((r + 1) * cols, 16), cols), :] = three_wide(x)
+            put_taps(change(ref[r].astype(jnp.float32)), dst, r + offset)
             return carry
+
         lax.fori_loop(0, rows, body, 0)
-    def widen_rims(i, dst, change):
+
+    def widen_rims(i, dst):
         for side in range(2):
             if remote:
                 copies[2 * i + side].wait_recv()
-            x = change(rims[i, side].astype(jnp.float32))
-            x = jnp.where(has[side], x, 0.0)
-            dst[pl.ds(side * (rows + 1) * cols, cols), :] = three_wide(x)
-    cells = rows * cols
-    def gradient(layer):
-        def body(dr, carry):
-            start = pl.multiple_of(dr * cols, 16)
-            for lane in range(0, 3 * n, 256):
-                size = min(256, 3 * n - lane)
-                part = jnp.dot(g_t[...], wide[pl.ds(start, cells), pl.ds(lane, size)],
-                               preferred_element_type=jnp.float32)
-                o_ref[layer, pl.ds(pl.multiple_of(dr * 3 * n + lane, 8), size), :] = part.T
-            return carry
-        lax.fori_loop(0, 3, body, 0)
-    for dr in range(3):
-        for seg in range(3):
-            tap = w_ref[pl.ds((3 * dr + 2 - seg) * n, n), :]
-            w_t[dr, pl.ds(seg * n, n), :] = tap.T
-    widen_rows(v_ref, wide, silu)
-    widen_rows(g_ref, wide_g, same)
-    g_t[...] = g_ref[...].T
-    widen_rims(0, wide_g, same)
-    widen_rims(1, wide, silu)
-    gradient(1)
-    half = cells // 2
+            put_taps(jnp.where(has[side], rims[i, side].astype(jnp.float32), 0.0), dst, side * (rows + 1))
+
+    def tap_rows(layer, d, cells, first):
+        o_ref[layer, pl.ds(pl.multiple_of(d * 3 * n, 8), 3 * n), :] = jnp.dot(
+            cells, g_n[pl.ds(pl.multiple_of(first, LANES), span), :], preferred_element_type=jnp.float32
+        )
+
+    widen_rows(g_ref, wide_g, same, 1)
+    g_n[pl.ds(LANES, span), :] = wide_g[n:2 * n, LANES:LANES + span].T
+    widen_rows(v_ref, wide_v, silu, 0)
+    tap_rows(1, 1, wide_v[...], LANES)
+    widen_rows(a_ref, wide_a, same, 1)
+    for d in range(3):
+        for s in range(3):
+            t = 3 * d + 2 - s
+            w_l[d, :, s * n:(s + 1) * n] = w_ref[:, t * n:(t + 1) * n].T
+    widen_rims(0, wide_g)
+    for row in (0, rows + 1):
+        g_n[pl.ds(row * LANES, LANES), :] = wide_g[n:2 * n, row * LANES:(row + 1) * LANES].T
+
+    def outer_taps(i, carry):
+        tap_rows(1, 2 * i, wide_v[...], (2 - 2 * i) * LANES)
+        return carry
+
+    lax.fori_loop(0, 2, outer_taps, 0)
+    half = span // 2
+
     def back_body(i, carry):
-        first = pl.multiple_of(i * half, 16)
         total = None
-        for dr in range(3):
-            x = wide_g[pl.ds(pl.multiple_of(first + (2 - dr) * cols, 16), half), :]
-            y = jnp.dot(x, w_t[dr], preferred_element_type=jnp.float32)
+        for d in range(3):
+            lanes = pl.ds(pl.multiple_of(i * half + (2 - d) * LANES, LANES), half)
+            y = jnp.dot(w_l[d], wide_g[:, lanes], preferred_element_type=jnp.float32)
             total = y if total is None else total + y
-        v = v_ref[pl.ds(first, half), :].astype(jnp.float32)
+        back[:, pl.ds(pl.multiple_of(i * half, LANES), half)] = total
+        return carry
+
+    lax.fori_loop(0, 2, back_body, 0)
+
+    def slope_body(r, carry):
+        v = v_ref[r].astype(jnp.float32)
         s = jax.nn.sigmoid(v)
-        back[pl.ds(first, half), :] = (total * (s * (1.0 + v * (1.0 - s)))).astype(jnp.bfloat16)
+        start = pl.multiple_of(r * LANES, LANES)
+        g0 = back[:, pl.ds(start, LANES)] * widened(s * (1.0 + v * (1.0 - s)))
+        g_n[pl.ds(pl.multiple_of(start + LANES, LANES), LANES), :] = g0.astype(jnp.bfloat16).T
         return carry
-    lax.fori_loop(0, 2, back_body, 0)
-    g_t[...] = back[...].T
-    widen_rows(a_ref, wide, same)
-    widen_rims(2, wide, same)
-    gradient(0)
+
+    lax.fori_loop(0, rows, slope_body, 0)
+    widen_rims(1, wide_a)
+
+    def first_taps(d, carry):
+        tap_rows(0, d, wide_a[:, pl.ds(pl.multiple_of(d * LANES, LANES), span)], LANES)
+        return carry
+
+    lax.fori_loop(0, 3, first_taps, 0)
     for copy in copies:
         copy.wait_send()
 
 def gradients(inputs, preacts, cotangent, weights, remote=True, collective_id=3):
     rows, cols, n = inputs.shape
-    flat = [x.reshape(rows * cols, n) for x in (inputs, preacts, cotangent)]
+    turned = [jnp.swapaxes(x, -1, -2) for x in (inputs, preacts, cotangent, weights)]
     b16 = jnp.bfloat16
-    return pl.pallas_call(functools.partial(grads_kernel, remote, rows, cols),
+    return pl.pallas_call(functools.partial(grads_kernel, remote),
         out_shape=jax.ShapeDtypeStruct((2, 9 * n, n), jnp.float32),
         in_specs=[pl.BlockSpec(memory_space=pltpu.VMEM)] * 4, out_specs=pl.BlockSpec(memory_space=pltpu.VMEM),
-        scratch_shapes=[pltpu.VMEM((3, 2, cols, n), b16), pltpu.VMEM(((rows + 2) * cols, 3 * n), b16),
-                        pltpu.VMEM(((rows + 2) * cols, 3 * n), b16), pltpu.VMEM((rows * cols, n), b16),
-                        pltpu.VMEM((n, rows * cols), b16), pltpu.VMEM((3, 3 * n, n), b16),
-                        pltpu.SemaphoreType.DMA((6,)), pltpu.SemaphoreType.DMA((6,))],
-        compiler_params=kernel_params(collective_id if remote else None))(*flat, weights)
+        scratch_shapes=[pltpu.VMEM((2, 2, n, cols), b16), pltpu.VMEM((3 * n, rows * LANES), b16),
+                        pltpu.VMEM((3 * n, (rows + 2) * LANES), b16), pltpu.VMEM((3 * n, (rows + 2) * LANES), b16),
+                        pltpu.VMEM((n, rows * LANES), jnp.float32), pltpu.VMEM(((rows + 2) * LANES, n), b16),
+                        pltpu.VMEM((3, n, 3 * n), b16), pltpu.SemaphoreType.DMA((4,)), pltpu.SemaphoreType.DMA((4,))],
+        compiler_params=kernel_params(collective_id if remote else None))(*turned)
 
 
 NB = 64
@@ -569,16 +594,20 @@
 
     def place_rows(block, carry):
         z, y_high = block // 2, block % 2
-        for q in range(8):
-            place = (q // 2, y_high * 2 + q % 2, z)
-            for p in range(3):
-                row = 48 * q + 16 * p
-                size = min(16, share - row)
-                if size <= 0:
-                    continue
-                a1, a2, a3 = ORDERS[p]
-                src = pl.multiple_of(((place[a1] * 4 + place[a2]) * 4 + place[a3]) * 16, 16)
-                dense[pl.ds(pl.multiple_of(block * share + row, 8), size), :] = in_ref[layer, p, pl.ds(src, size), :]
+        for pair in range(4):
+            loaded = []
+            for q in (2 * pair, 2 * pair + 1):
+                place = (q // 2, y_high * 2 + q % 2, z)
+                for p in range(3):
+                    row = 48 * q + 16 * p
+                    size = min(16, share - row)
+                    if size <= 0:
+                        continue
+                    a1, a2, a3 = ORDERS[p]
+                    src = pl.multiple_of(((place[a1] * 4 + place[a2]) * 4 + place[a3]) * 16, 16)
+                    loaded.append((row, size, in_ref[layer, p, pl.ds(src, size), :]))
+            for row, size, value in loaded:
+                dense[pl.ds(pl.multiple_of(block * share + row, 8), size), :] = value
         return carry
 
     lax.fori_loop(0, 8, place_rows, 0)

time: 239 us -> 220 us (0.921)
  Pallas kernels: 216 us -> 204 us
  local copies, waits for them, and re-layouts: 17.7 us -> 10.7 us
    pallas_call x1, Pallas kernels: 45.7 us -> 37.9 us  [gradients(): pl.pallas_call(functools.partial(grads_kernel, remote), out_shape=jax.Sha...]
    unnamed x17 -> x19, local copies, waits for them, and re-layouts: 15.2 us -> 8.2 us
    pallas_call x1, Pallas kernels: 79.5 us -> 76.2 us  [reduce_all(): pl.pallas_call(reduce_kernel, out_shape=jax.ShapeDtypeStruct(g.shape, jnp...]
where the time goes in v5:
time: 220 us
  Pallas kernels  204 us (93%)
  local copies, waits for them, and re-layouts  10.7 us (5%)
  matrix products  4.4 us (2%)
    pallas_call x1, Pallas kernels, reduce_all(): pl.pallas_call(reduce_kernel, out_shape=jax.ShapeDtypeStruct(g.shape, jnp...  76.2 us
    pallas_call x1, Pallas kernels, gram_of_rows(): pl.pallas_call(gram_kernel, out_shape=(jax.ShapeDtypeStruct((3, 256, n),...  40.8 us
    pallas_call x1, Pallas kernels, gradients(): pl.pallas_call(functools.partial(grads_kernel, remote), out_shape=jax.Sha...  37.9 us
    pallas_call x1, Pallas kernels, factor(): pl.pallas_call(factor_kernel, out_shape=(jax.ShapeDtypeStruct((2, 3, 1024...  35.8 us
    pallas_call x1, Pallas kernels, basis_of(): pl.pallas_call(functools.partial(basis_kernel, full_rows), grid=(2,), out...  13.4 us
    unnamed x19, local copies, waits for them, and re-layouts  8.2 us

profile of v5, /device:TPU:1, one launch (start us, length us, event | category | flops | bytes accessed | tf_op | source)
XLA Modules:
  0.0 220.0 jit_solution(11111472558576236148)
XLA Ops:
  0.6 0.0 copy-start
  0.7 0.0 copy-start.2
  0.7 1.4 copy-done.2
  2.0 0.0 copy-start.3
  2.0 1.3 copy-done.3
  3.3 0.0 copy-start.4
  3.3 1.3 copy-done.4
  4.7 37.9 %shard_map.111.g_ref = f32[2,2880,320]{2,1,0:T(8,128)} custom-call(bf16[8,320,240]{2,1,0:T(8,128)(2,1)S(1)} %bitcast.18, bf16[8,320,240]{2,1,0:T(8,128)(2,1)S(1)} %bitcast.19, bf16[8,320,240]{2,1,0:T(8,128)(2,1)S(1)} %bitcast.20, bf16[320,2880]{1,0:T(8,128)(2,1)} %bitcast.22), custom_call_target="tpu_custom_call" | custom-call | tf_op jit(solution)/shard_map/pallas_call | solution.py:448
  42.6 0.0 copy-start.8
  42.6 76.2 %shard_map.112.g_ref = f32[2,2880,320]{2,1,0:T(8,128)} custom-call(f32[2,2880,320]{2,1,0:T(8,128)} %shard_map.111.g_ref), custom_call_target="tpu_custom_call" | custom-call | tf_op jit(solution)/shard_map/pallas_call | solution.py:206
  118.8 0.0 copy-done.8
  118.8 3.0 %fusion = f32[2,360,180]{1,2,0:T(8,128)S(1)} fusion(f32[2,2880,320]{2,1,0:T(8,128)} %shard_map.112.g_ref, s32[]{:T(128)S(6)} %select_n.6, f32[2,360,180]{1,0,2:T(2,128)S(1)} %copy-done.8, s32[]{:T(128)S(6)} %select_n.7), kind=kOutput, calls=%fused_computation.1 | convolution fusion | flops 498052800 | bytes 2707976 | tf_op jit(solution)/shard_map/dot_general | solution.py:650
  121.8 1.1 copy.16
  122.9 0.0 copy-done
  122.9 0.0 copy-start.6
  122.9 0.0 copy-start.7
  122.9 1.4 fusion.2
  124.3 1.1 pad.4.p_ref
  125.4 0.0 copy-done.6
  125.4 0.0 copy-done.7
  125.4 40.8 %shard_map.113 = (f32[3,256,320]{2,1,0:T(8,128)}, f32[384,320]{1,0:T(8,128)S(1)}, f32[320,320]{1,0:T(8,128)S(1)}, f32[320,320]{1,0:T(8,128)S(1)}, f32[320,320]{1,0:T(8,128)S(1)}) custom-call(f32[2,384,320]{2,1,0:T(8,128)} %pad.4.p_ref, f32[2,2880,320]{2,1,0:T(8,128)} %shard_map.112.g_ref, f32[2,320,320]{2,1,0:T(8,128)S(1)} %copy-done.6, ...), custom_call_target="tpu_custom_call" | custom-call | tf_op jit(solution)/shard_map/pallas_call | solution.py:329
  166.3 0.0 copy-start.5
  166.3 1.3 copy-done.5
  167.5 35.8 %shard_map.114 = (f32[2,3,1024,320]{3,2,1,0:T(8,128)}, f32[2,3,320,320]{3,2,1,0:T(8,128)}) custom-call(f32[3,256,320]{2,1,0:T(8,128)S(1)} %copy-done.5, f32[384,320]{1,0:T(8,128)S(1)} %get-tuple-element.12.gram_ref, f32[320,320]{1,0:T(8,128)S(1)} %get-tuple-element.13.right_ref, f32[320,320]{1,0:T(8,128)S(1)} %get-tuple-element.14.rows_ref, ...), custom_call_target="tpu_custom_call" | custom-call | tf_op jit(solution)/shard_map/pallas_call | solution.py:581
  203.3 0.0 copy-start.1
  203.3 1.8 copy-done.1
  205.1 13.4 %shard_map.115 = f32[2,320,2880]{2,1,0:T(8,128)} custom-call(f32[2,3,1024,320]{3,2,1,0:T(8,128)} %get-tuple-element.16.in_ref, f32[2,3,320,320]{3,2,1,0:T(8,128)S(1)} %copy-done.1), custom_call_target="tpu_custom_call" | custom-call | tf_op jit(solution)/shard_map/pallas_call | solution.py:629
  218.6 1.4 slice_bitcast_fusion
Async XLA Ops:
  0.6 122.2 %copy-start = (f32[2,180,320]{2,0,1:T(2,128)S(1)}, f32[2,180,320]{2,0,1:T(2,128)}, u32[]{:S(2)}) copy-start(f32[2,180,320]{2,0,1:T(2,128)} %param.13) | copy-start | bytes 1382404
  0.7 1.4 copy-start.2
  2.0 1.3 copy-start.3
  3.3 1.3 copy-start.4
  42.6 76.2 %copy-start.8 = (f32[2,360,180]{1,0,2:T(2,128)S(1)}, f32[2,360,180]{1,0,2:T(2,128)}, u32[]{:S(2)}) copy-start(f32[2,360,180]{1,0,2:T(2,128)} %param.12) | copy-start | bytes 1555204
  122.9 2.6 %copy-start.6 = (f32[2,320,320]{2,1,0:T(8,128)S(1)}, f32[2,320,320]{2,1,0:T(8,128)}, u32[]{:S(2)}) copy-start(f32[2,320,320]{2,1,0:T(8,128)} %rs_ref.1) | copy-start | bytes 2457604
  122.9 2.6 %copy-start.7 = (f32[2,320,320]{2,1,0:T(8,128)S(1)}, f32[2,320,320]{2,1,0:T(8,128)}, u32[]{:S(2)}) copy-start(f32[2,320,320]{2,1,0:T(8,128)} %rb_ref.1) | copy-start | bytes 2457604
  166.3 1.3 copy-start.5
  203.3 1.8 copy-start.1
